TPU v7x, 32 devices: a whole 2x2x4 slice. The times are simulated.
32 devices in a mesh: doc: 8 (over z, x), vocab: 4 (over y, core).
Axes of the slice: x: 2, y: 2, z: 4, core: 2. Of those that a mesh axis runs over, the one named last changes fastest.
Arguments:
- count_tiles: int32 [32, 32, 2, 16, 128], P(('doc', 'vocab')), may hold values from 0 to 3
- tile_words: int32 [32, 32, 2], P(('doc', 'vocab')), may hold values from 0 to 31
- whitening: bfloat16 [131072, 512], P(('doc', 'vocab')), may hold values from -0.08 to 0.16
- seeds: int32 [512], replicated, may hold values from 0 to 511, as said below
Outputs:
- topic_directions: float32 [512, 512], P('vocab')
- topic_weights: float32 [512], replicated
Inputs may be any that keep to these rules, and one draw needn't show every extreme that they name: `seeds`: 512 distinct document indices; the first and the last document are among them.
All inputs are finite; a program needn't handle non-finite values.
Results may differ from a plain program's by a relative error of at most 0.0003.
Values sent between devices are 32-bit elements; how exact they have to be, the bound alone decides.
No kernel may reach another device: no remote copies, remote signals or barrier semaphores. Data moves between devices by JAX's collectives and lax.ppermute only.
A program may use at most 128 MiB of HBM per device.

v0:
```python
import math

import jax
import jax.numpy as jnp
from jax import lax
from jax.sharding import PartitionSpec as P

ITERS = 2
SWEEPS = 4


SHIFT = 2.0
EPS = 1e-06
HIGHEST = lax.Precision.HIGHEST


def inner_rows(left, right):
    return lax.dot_general(
        left, right, (((0,), (0,)), ((), ())), precision=HIGHEST, preferred_element_type=jnp.float32
    )


def block_terms(tiles_part, words_part, word_table):
    picked = jnp.take(word_table, words_part, axis=0)
    return jnp.einsum(
        "btdw,btwk->bdk",
        tiles_part.astype(jnp.bfloat16),
        picked,
        preferred_element_type=jnp.float32,
    )


def partial_rows(tiles_local, words_local, word_table, block_count):
    group_size = math.gcd(block_count, 16)

    def one_group(turn_index):
        block_start = turn_index * group_size
        tiles_part = lax.dynamic_slice_in_dim(tiles_local, block_start, group_size, 0)
        words_part = lax.dynamic_slice_in_dim(words_local, block_start, group_size, 0)
        return block_terms(tiles_part, words_part, word_table)

    stacked = lax.map(one_group, jnp.arange(block_count // group_size, dtype=jnp.int32))
    return stacked.reshape(-1, word_table.shape[2])


def polar_sweeps(moment, current, sweeps):
    topics = current.shape[0]
    shift_scale = topics * jnp.sqrt(jnp.mean(moment * moment) + EPS)
    iterate = (moment + SHIFT * shift_scale * current) / ((SHIFT + 1.0) * shift_scale)
    for sweep_number in range(sweeps):
        gram_matrix = inner_rows(iterate, iterate)
        iterate = 1.5 * iterate - 0.5 * jnp.dot(
            iterate, gram_matrix, precision=HIGHEST, preferred_element_type=jnp.float32
        )
    return iterate


def orthonormal(moment_part, current):
    moment = lax.psum(moment_part, ("doc", "vocab"))
    return polar_sweeps(moment, current, SWEEPS)


def per_device(count_tiles, tile_words, whitening, seeds):
    tiles_local = count_tiles[0]
    words_local = tile_words[0]
    doc_dev = tiles_local.shape[2]
    word_block = tiles_local.shape[3]
    topics = whitening.shape[1]
    word_table = whitening.reshape(-1, word_block, topics)
    owned = lax.psum_scatter(
        partial_rows(
            tiles_local,
            words_local,
            word_table,
            doc_dev * lax.axis_size(("doc", "vocab")) // doc_dev,
        ),
        ("doc", "vocab"),
        scatter_dimension=0,
        tiled=True,
    )
    first_doc = lax.axis_index(("doc", "vocab")) * doc_dev
    seed_hits = (
        seeds[None, :] == first_doc + jnp.arange(doc_dev, dtype=jnp.int32)[:, None]
    ).astype(jnp.float32)
    current = orthonormal(inner_rows(owned, seed_hits), jnp.eye(topics, dtype=jnp.float32))
    for step_number in range(ITERS):
        projected = jnp.dot(owned, current, precision=HIGHEST, preferred_element_type=jnp.float32)
        current = orthonormal(inner_rows(owned, projected * projected), current)
    projected = jnp.dot(owned, current, precision=HIGHEST, preferred_element_type=jnp.float32)
    cube_total = lax.psum(jnp.sum(projected * projected * projected, axis=0), ("doc", "vocab"))
    weights = cube_total / (doc_dev * lax.axis_size(("doc", "vocab")))
    own_rows = topics // lax.axis_size("vocab")
    directions = lax.dynamic_slice_in_dim(
        current, lax.axis_index("vocab") * own_rows, own_rows, 0
    ) * math.sqrt(topics)
    return (directions, weights)


def solution(mesh):
    in_specs = (
        P(("doc", "vocab"), None, None, None, None),
        P(("doc", "vocab"), None, None),
        P(("doc", "vocab"), None),
        P(),
    )
    out_specs = (P("vocab", None), P())
    return jax.shard_map(
        per_device, mesh=mesh, in_specs=in_specs, out_specs=out_specs, check_vma=False
    )
```

profile of v0, /device:TPU:0, one launch (start us, length us, event | category | flops | bytes accessed | tf_op | source)
XLA Modules:
  0.0 680.7 jit_solution(1562998445026471034)
XLA Ops:
  7.2 20.4 %while.10 = (s32[]{:T(128)}, f32[2,16,16,512]{3,2,1,0:T(8,128)S(1)}, s32[2]{0:T(128)S(1)}, s32[32,2,16,128]{3,2,1,0:T(8,128)}, s32[32,2]{0,1:T(2,128)}, /*index=...) while((s32[]{:T(128)}, f32[2,16,16,512]{3,2,1,0:T(8,128)S(1)}, ...), condition=%wide.region_1.2_spmd, body=%wide.region_0.1_spmd.sunk | while | flops 69272872 | bytes 15474279 | solution.py:42
  9.5 5.0 gather_fusion
  14.5 3.0 fusion.98
  19.6 5.0 gather_fusion
  24.6 3.0 fusion.98
  28.7 137.5 %reduce-scatter.2.cloned.1.call-done = f32[16,512]{1,0:T(8,128)} async-done(((f32[512,512]{1,0:T(8,128)}), f32[16,512]{1,0:T(8,128)}) %reduce-scatter.2.cloned.1.call-update) | async-done | bytes 32784 | tf_op jit(solution)/shard_map/reduce_scatter | solution.py:70
  166.2 2.4 fusion.26
  168.7 129.4 %all-reduce.4.cloned.1.call-done = f32[512,512]{1,0:T(8,128)} async-done(((f32[512,512]{1,0:T(8,128)}), f32[512,512]{1,0:T(8,128)}) %all-reduce.4.cloned.1.call-update) | async-done | bytes 1048592 | tf_op jit(solution)/shard_map/psum | solution.py:59
  298.1 2.2 multiply_reduce_fusion.2
  301.0 3.5 fusion.24
  304.5 1.9 fusion.23
  308.3 1.9 fusion.22
  313.9 13.5 %fusion.36 = f32[512,512]{1,0:T(8,128)S(1)} fusion(f32[512,512]{1,0:T(8,128)S(1)} %fusion.21), kind=kOutput, calls=%fused_computation.63 | convolution fusion | flops 1610612736 | bytes 2097152 | tf_op jit(solution)/shard_map/dot_general | solution.py:18
  327.4 1.9 fusion.20
  329.9 2.1 fusion.37
  332.0 128.9 %all-reduce.6.cloned.1.call-done = f32[512,512]{1,0:T(8,128)} async-done(((f32[512,512]{1,0:T(8,128)}), f32[512,512]{1,0:T(8,128)}) %all-reduce.6.cloned.1.call-update) | async-done | bytes 1048592 | tf_op jit(solution)/shard_map/psum | solution.py:59
  460.9 2.2 multiply_reduce_fusion.1
  463.8 3.6 fusion.32
  467.4 2.0 fusion.19
  469.5 1.9 fusion.38
  471.4 1.9 fusion.18
  475.2 1.9 fusion.17
  477.0 2.3 fusion.40
  481.8 2.1 fusion.41
  483.9 129.0 %all-reduce.8.cloned.1.call-done = f32[512,512]{1,0:T(8,128)} async-done(((f32[512,512]{1,0:T(8,128)}), f32[512,512]{1,0:T(8,128)}) %all-reduce.8.cloned.1.call-update) | async-done | bytes 1048592 | tf_op jit(solution)/shard_map/psum | solution.py:59
  612.9 2.2 multiply_reduce_fusion
  615.7 3.6 fusion.33
  619.3 2.0 fusion.15
  621.4 1.9 fusion.42
  623.3 2.1 fusion.14
  631.0 1.9 fusion.12
  633.5 39.2 %psum.31 = f32[512]{0:T(512)S(1)} all-reduce(f32[512]{0:T(512)S(1)} %fusion.25), channel_id=1, replica_groups=mesh['doc'=8,'vocab'=4] {'doc','vocab'}, use_global_device_ids=true, to_apply=%region_10.11 | all-reduce | flops 512 | bytes 4096 | tf_op jit(solution)/shard_map/psum | solution.py:90
  (54 shorter events, 22.4 us)
Async XLA Ops:
  7.2 159.1 %reduce-scatter.2.cloned.1.call-start = ((), (), s32[]{:S(2)}) async-start(), calls=%async_computation.1 | async-start | bytes 1081344 | tf_op jit(solution)/shard_map/reduce_scatter | solution.py:70
  7.2 159.0 %copy-start.5 = (s32[512]{0:T(512)S(1)}, s32[512]{0:T(512)}, u32[]{:S(2)}) copy-start(s32[512]{0:T(512)} %param.9) | copy-start | bytes 6148
  9.4 5.0 copy-start.6
  19.6 5.0 copy-start.6
  27.6 1.0 copy-start.4
  28.6 269.4 %all-reduce.4.cloned.1.call-start = ((), (), s32[]{:S(2)}) async-start(), calls=%async_computation.2 | async-start | bytes 2097152 | tf_op jit(solution)/shard_map/psum | solution.py:59
  168.7 292.3 %all-reduce.6.cloned.1.call-start = ((), (), s32[]{:S(2)}) async-start(), calls=%async_computation.3 | async-start | bytes 2097152 | tf_op jit(solution)/shard_map/psum | solution.py:59
  298.1 6.4 copy-start.3
  312.0 17.2 %copy-start = (f32[16,512]{1,0:T(8,128)S(1)}, f32[16,512]{1,0:T(8,128)}, u32[]{:S(2)}) copy-start(f32[16,512]{1,0:T(8,128)} %reduce-scatter.2.cloned.1.call-done) | copy-start | bytes 98308
  331.9 280.9 %all-reduce.8.cloned.1.call-start = ((), (), s32[]{:S(2)}) async-start(), calls=%async_computation.4 | async-start | bytes 2097152 | tf_op jit(solution)/shard_map/psum | solution.py:59
  460.9 6.5 copy-start.2
  612.9 6.5 copy-start.1
Sparse Core Ops, SparseCore 0:
  28.7 137.4 reduce-scatter.1
  172.2 125.7 all-reduce.3
  332.1 128.8 all-reduce.5
  484.0 128.7 all-reduce.7
where the time goes:
time: 685 us; the launch traced here: 681 us
  waiting for transfers between devices  525 us (77%)
  matrix products  76.9 us (11%)
  blocking collectives  39.2 us (6%)
  between operations  16.3 us (2%)
  local copies, waits for them, and re-layouts  14 us (2%)
  other arithmetic  7.91 us (1%)
    psum x3, waiting for transfers between devices, orthonormal(): moment = lax.psum(moment_part, ('doc', 'vocab'))  387 us
    reduce_scatter x1, waiting for transfers between devices, per_device(): lax.psum_scatter(partial_rows(tiles_local, words_local, word_table, doc_d...  138 us
    dot_general x15, matrix products, inner_rows(): lax.dot_general(left, right, (((0,), (0,)), ((), ())), precision=HIGHEST,...  46.1 us
    psum x1, blocking collectives, per_device(): lax.psum(jnp.sum(projected * projected * projected, axis=0), ('doc', 'voc...  39.2 us
    dot_general x12, matrix products, polar_sweeps(): jnp.dot(iterate, gram_matrix, precision=HIGHEST, preferred_element_type=j...  23 us
  transfers between devices with their start and end apart: 4, of which 4 were waited for; matrix products, arithmetic and copies ran while one was open for 0% of the time, Pallas kernels for 0%

commit v1 on v0

v1 whole, which is shorter than its diff:
```python
import functools
import math

import jax
import jax.numpy as jnp
from jax import lax
from jax.experimental import pallas as pl
from jax.experimental.pallas import tpu as pltpu
from jax.sharding import PartitionSpec as P

ITERS = 2
SWEEPS = 4
SHIFT = 2.0
EPS = 1e-06
AXES = ("doc", "vocab")
F32 = jnp.float32
BF16 = jnp.bfloat16
NN = (((1,), (0,)), ((), ()))
NT = (((1,), (1,)), ((), ()))


def split(value):
    high = value.astype(BF16)
    return high, (value - high.astype(F32)).astype(BF16)


def product(left, right, dims):
    left_high, left_low = split(left)
    right_high, right_low = split(right)
    dot = functools.partial(lax.dot_general, dimension_numbers=dims, preferred_element_type=F32)
    return dot(left_high, right_high) + (dot(left_high, right_low) + dot(left_low, right_high))


def plan(n_doc, n_vocab):
    n = n_doc * n_vocab
    bits = [1 << b for b in range(n.bit_length() - 1)]
    halving, whole = bits[:-2], bits[-2:]
    pairs = [(b, b) for b in halving]
    if len(halving) >= 3:
        pairs[1], pairs[2] = (halving[2], halving[1]), (halving[1], halving[2])
    return pairs, [(b, b) for b in whole]


def unit_at(place, me, pairs):
    steps = len(pairs)
    top = (place >> (steps - 1)) & 1
    odd = (me & 1) ^ top
    unit = (me & ((1 << steps) - 1)) ^ top
    for s in range(1, steps):
        even_mask, odd_mask = pairs[s]
        mask = even_mask + odd * (odd_mask - even_mask)
        unit = unit ^ (((place >> (steps - 1 - s)) & 1) * mask)
    return unit


def exchange(value, masks, n):
    perm = [(i, i ^ masks[i & 1]) for i in range(n)]
    return lax.ppermute(value, AXES, perm)


def whiten_kernel(pairs, unit_blocks, half_blocks, step_blocks, me_ref, words, tiles, table, keep, send, dense):
    step = pl.program_id(0)
    me = me_ref[0]
    doc_dev, word_block = tiles.shape[2], tiles.shape[3]
    dense[...] = jnp.zeros_like(dense)
    for local in range(2 * step_blocks):
        inside = local % step_blocks
        block_place = step * step_blocks + inside + (half_blocks if local >= step_blocks else 0)
        unit = unit_at(block_place // unit_blocks, me, pairs)
        block = unit * unit_blocks + block_place % unit_blocks
        rows = pl.ds(local * doc_dev, doc_dev)
        for t in range(tiles.shape[1]):
            columns = pl.ds(pl.multiple_of(words[block, t] * word_block, word_block), word_block)
            dense[rows, columns] = dense[rows, columns] + tiles[block, t].astype(F32).astype(BF16)
    rows = step_blocks * doc_dev
    send[...] = jnp.dot(dense[rows:, :], table[...], preferred_element_type=F32)
    keep[...] = jnp.dot(dense[:rows, :], table[...], preferred_element_type=F32)


def partial_rows(tiles, words, table, me, pairs):
    blocks, _, doc_dev, _ = tiles.shape
    topics = table.shape[1]
    unit_blocks = blocks >> len(pairs)
    half_blocks = blocks // 2
    step_blocks = math.gcd(half_blocks, 16)
    step_rows = step_blocks * doc_dev
    half = jax.ShapeDtypeStruct((half_blocks * doc_dev, topics), F32)
    out = pl.BlockSpec((step_rows, topics), lambda i: (i, 0))
    return pl.pallas_call(
        functools.partial(whiten_kernel, pairs, unit_blocks, half_blocks, step_blocks),
        grid=(half_blocks // step_blocks,),
        in_specs=[
            pl.BlockSpec(memory_space=pltpu.SMEM),
            pl.BlockSpec(memory_space=pltpu.SMEM),
            pl.BlockSpec(memory_space=pltpu.VMEM),
            pl.BlockSpec(memory_space=pltpu.VMEM),
        ],
        out_specs=[out, out],
        out_shape=[half, half],
        scratch_shapes=[pltpu.VMEM((2 * step_rows, table.shape[0]), BF16)],
        compiler_params=pltpu.CompilerParams(vmem_limit_bytes=40 << 20),
        name="whiten",
    )(me, words, tiles, table)


def iterate_kernel(chunk, docs_ref, seeds_ref, white_ref, basis_ref, weights_ref, moment_ref):
    topics = basis_ref.shape[0]
    docs = white_ref.shape[0]
    chunks = docs // chunk

    def rows_of(i):
        return pl.ds(pl.multiple_of(i * chunk, chunk), chunk)

    def projected(i):
        return product(basis_ref[...], white_ref[rows_of(i), :], NT)

    row = lax.broadcasted_iota(jnp.int32, (topics, topics), 0)
    column = lax.broadcasted_iota(jnp.int32, (topics, topics), 1)
    basis_ref[...] = jnp.where(row == column, 1.0, 0.0).astype(F32)

    def turn(number, carry):
        moment_ref[...] = jnp.zeros_like(moment_ref)

        def add(i, carry):
            @pl.when(number == 0)
            def _():
                hits = (seeds_ref[...] == docs_ref[i]).astype(F32).astype(BF16)
                high, low = split(white_ref[rows_of(i), :])
                moment_ref[...] += jnp.dot(hits, high, preferred_element_type=F32) + jnp.dot(
                    hits, low, preferred_element_type=F32
                )

            @pl.when(number > 0)
            def _():
                value = projected(i)
                moment_ref[...] += product(value * value, white_ref[rows_of(i), :], NN)

            return carry

        lax.fori_loop(0, chunks, add, 0)
        moment = moment_ref[...]
        scale = topics * jnp.sqrt(jnp.mean(moment * moment) + EPS)
        basis_ref[...] = (moment + SHIFT * scale * basis_ref[...]) / ((SHIFT + 1.0) * scale)

        def sweep(_, carry):
            current = basis_ref[...]
            gram = product(current, current, NT)
            basis_ref[...] = 1.5 * current - 0.5 * product(gram, current, NN)
            return carry

        lax.fori_loop(0, SWEEPS, sweep, 0)
        return carry

    lax.fori_loop(0, ITERS + 1, turn, 0)
    weights_ref[...] = jnp.zeros_like(weights_ref)

    def cubes(i, carry):
        value = projected(i)
        weights_ref[...] += jnp.sum(value * value * value, axis=1, keepdims=True)
        return carry

    lax.fori_loop(0, chunks, cubes, 0)
    weights_ref[...] = weights_ref[...] / docs


def iterate(white, docs_row, seeds):
    docs, topics = white.shape
    chunk = math.gcd(docs, 512)
    vmem = pl.BlockSpec(memory_space=pltpu.VMEM)
    return pl.pallas_call(
        functools.partial(iterate_kernel, chunk),
        in_specs=[vmem] * 3,
        out_specs=[vmem] * 2,
        out_shape=[
            jax.ShapeDtypeStruct((topics, topics), F32),
            jax.ShapeDtypeStruct((topics, 1), F32),
        ],
        scratch_shapes=[pltpu.VMEM((topics, topics), F32)],
        compiler_params=pltpu.CompilerParams(vmem_limit_bytes=40 << 20),
        name="iterate",
    )(docs_row.reshape(docs // chunk, 1, chunk), seeds.reshape(topics, 1), white)


def per_device(n_doc, n_vocab, count_tiles, tile_words, whitening, seeds):
    n = n_doc * n_vocab
    pairs, whole = plan(n_doc, n_vocab)
    me = lax.axis_index(AXES).astype(jnp.int32)
    keep, send = partial_rows(count_tiles[0], tile_words[0], whitening, me.reshape(1), pairs)
    docs, topics = keep.shape[0] * 2, keep.shape[1]
    unit_rows = docs >> len(pairs)
    value = keep + exchange(send, pairs[0], n)
    for masks in pairs[1:]:
        half = value.shape[0] // 2
        value = value[:half] + exchange(value[half:], masks, n)
    for masks in whole:
        value = value + exchange(value, masks, n)
    for masks in reversed(pairs):
        value = jnp.concatenate([value, exchange(value, masks, n)])
    place = jnp.arange(docs, dtype=jnp.int32)
    docs_row = unit_at(place // unit_rows, me, pairs) * unit_rows + place % unit_rows
    basis, weights = iterate(value, docs_row, seeds)
    own_rows = topics // n_vocab
    own = lax.dynamic_slice_in_dim(basis, lax.axis_index("vocab") * own_rows, own_rows, 1)
    return own.T * math.sqrt(topics), weights.reshape(topics)


def solution(mesh):
    in_specs = (
        P(("doc", "vocab"), None, None, None, None),
        P(("doc", "vocab"), None, None),
        P(("doc", "vocab"), None),
        P(),
    )
    out_specs = (P("vocab", None), P())
    return jax.shard_map(
        functools.partial(per_device, mesh.shape["doc"], mesh.shape["vocab"]),
        mesh=mesh,
        in_specs=in_specs,
        out_specs=out_specs,
        check_vma=False,
    )
```

time: 685 us -> 82 us (0.12)
  waiting for transfers between devices: 525 us -> 26.7 us
  matrix products: 76.9 us -> 0 us
  blocking collectives: 39.2 us -> 0 us
  Pallas kernels: 0 us -> 33.7 us
  between operations: 16.3 us -> 0.74 us
  starting transfers between devices: 0.16 us -> 14.6 us
  local copies, waits for them, and re-layouts: 14 us -> 5 us
    psum x3 -> x0, waiting for transfers between devices: 387 us -> none  [orthonormal(): moment = lax.psum(moment_part, ('doc', 'vocab'))]
    reduce_scatter x1 -> x0, waiting for transfers between devices: 138 us -> none  [per_device(): lax.psum_scatter(partial_rows(tiles_local, words_local, word_table, doc_d...]
    dot_general x32 -> x0, matrix products: 76.9 us -> none  [the longest x15 46.1 us: inner_rows(): lax.dot_general(left, right, (((0,), (0,)), ((), ())), precision=HIGHEST,...]
    psum x1 -> x0, blocking collectives: 39.2 us -> none  [per_device(): lax.psum(jnp.sum(projected * projected * projected, axis=0), ('doc', 'voc...]
    pallas_call x0 -> x2, Pallas kernels: none -> 33.7 us  [the longest x1 29.9 us: iterate(): pl.pallas_call(functools.partial(iterate_kernel, chunk), in_specs=[vmem]...]
    ppermute x0 -> x8, waiting for transfers between devices: none -> 26.7 us  [exchange(): return lax.ppermute(value, AXES, perm)]
    ppermute x0 -> x8, starting transfers between devices: none -> 14.6 us  [exchange(): return lax.ppermute(value, AXES, perm)]
    gather x2 -> x0, local copies, waits for them, and re-layouts: 9.97 us -> none  [block_terms(): picked = jnp.take(word_table, words_part, axis=0)]
  transfers between devices with their start and end apart: 4 -> 8, of which waited for: 4 -> 8; matrix products, arithmetic and copies ran while one was open for 0% -> 0% of each run, Pallas kernels for 0% -> 0%
where the time goes in v1:
time: 82 us; the launch traced here: 81.8 us
  Pallas kernels  33.7 us (41%)
  waiting for transfers between devices  26.7 us (33%)
  starting transfers between devices  14.6 us (18%)
  local copies, waits for them, and re-layouts  5 us (6%)
  other arithmetic  1.09 us (1%)
    pallas_call x1, Pallas kernels, iterate(): pl.pallas_call(functools.partial(iterate_kernel, chunk), in_specs=[vmem]...  29.9 us
    ppermute x8, waiting for transfers between devices, exchange(): return lax.ppermute(value, AXES, perm)  26.7 us
    ppermute x8, starting transfers between devices, exchange(): return lax.ppermute(value, AXES, perm)  14.6 us
    unnamed x7, local copies, waits for them, and re-layouts  4.07 us
    pallas_call x1, Pallas kernels, partial_rows(): pl.pallas_call(functools.partial(whiten_kernel, pairs, unit_blocks, half_...  3.74 us
  transfers between devices with their start and end apart: 8, of which 8 were waited for; matrix products, arithmetic and copies ran while one was open for 0% of the time, Pallas kernels for 0%

profile of v1, /device:TPU:0, one launch (start us, length us, event | category | flops | bytes accessed | tf_op | source)
XLA Modules:
  0.0 81.8 jit_solution(1730745716902105375)
XLA Ops:
  0.6 0.8 copy.8.words
  1.4 0.0 copy-start
  1.4 2.2 %copy-done = bf16[4096,512]{1,0:T(8,128)(2,1)S(1)} copy-done((bf16[4096,512]{1,0:T(8,128)(2,1)S(1)}, bf16[4096,512]{1,0:T(8,128)(2,1)}, u32[]{:S(2)}) %copy-start) | copy-done | bytes 4194328
  3.6 0.0 copy-start.1
  3.6 1.0 %copy-done.1 = s32[1,32,2,16,128]{4,3,2,1,0:T(8,128)S(1)} copy-done((s32[1,32,2,16,128]{4,3,2,1,0:T(8,128)S(1)}, s32[1,32,2,16,128]{4,3,2,1,0:T(8,128)}, u32[]{:S(2)}) %copy-start.1) | copy-done | bytes 524312
  4.6 0.0 copy-start.2
  4.6 3.7 %whiten.1 = (f32[256,512]{1,0:T(8,128)S(1)}, f32[256,512]{1,0:T(8,128)S(1)}) custom-call(s32[1]{0:T(128)} %bitcast.1.me_ref, s32[32,2]{1,0:T(8,128)S(1)} %copy.8.words, s32[32,2,16,128]{3,2,1,0:T(8,128)S(1)} %bitcast.6, bf16[4096,512]{1,0:T(8,128)(2,1)S(1)} %copy-done), custom_call_target="tpu_custom_call" | custom-call | tf_op jit(solution)/shard_map/whiten/pallas_call | solution.py:89
  8.4 0.5 collective-permute-start
  8.9 1.5 %collective-permute-done = f32[256,512]{1,0:T(8,128)S(1)} collective-permute-done((f32[256,512]{1,0:T(8,128)S(1)}, f32[256,512]{1,0:T(8,128)S(1)}, u32[]{:S(2)}, u32[]{:S(2)}) %collective-permute-start) | collective-permute-done | bytes 524320 | tf_op jit(solution)/shard_map/ppermute | solution.py:58
  10.4 0.1 add.81
  10.5 2.9 %collective-permute-start.1 = (f32[128,512]{1,0:T(8,128)S(1)}, f32[128,512]{1,0:T(8,128)S(1)}, u32[]{:S(2)}, u32[]{:S(2)}) collective-permute-start(f32[128,512]{1,0:T(8,128)S(1)} %slice.17), channel_id=1, source_target_pairs={{0,4},{1,3},{2,6},{3,1},{4,0},{5,7},{6,2},{7,5},{8,12},{9,11},{10,... | collective-permute-start | bytes 786440 | tf_op jit(solution)/shard_map/ppermute | solution.py:58
  13.5 4.4 %collective-permute-done.1 = f32[128,512]{1,0:T(8,128)S(1)} collective-permute-done((f32[128,512]{1,0:T(8,128)S(1)}, f32[128,512]{1,0:T(8,128)S(1)}, u32[]{:S(2)}, u32[]{:S(2)}) %collective-permute-start.1) | collective-permute-done | bytes 262176 | tf_op jit(solution)/shard_map/ppermute | solution.py:58
  17.9 2.1 %collective-permute-start.2 = (f32[64,512]{1,0:T(8,128)S(1)}, f32[64,512]{1,0:T(8,128)S(1)}, u32[]{:S(2)}, u32[]{:S(2)}) collective-permute-start(f32[64,512]{1,0:T(8,128)S(1)} %slice.19), channel_id=1, source_target_pairs={{0,2},{1,5},{2,0},{3,7},{4,6},{5,1},{6,4},{7,3},{8,10},{9,13},{10,... | collective-permute-start | bytes 393224 | tf_op jit(solution)/shard_map/ppermute | solution.py:58
  20.0 2.9 %collective-permute-done.2 = f32[64,512]{1,0:T(8,128)S(1)} collective-permute-done((f32[64,512]{1,0:T(8,128)S(1)}, f32[64,512]{1,0:T(8,128)S(1)}, u32[]{:S(2)}, u32[]{:S(2)}) %collective-permute-start.2) | collective-permute-done | bytes 131104 | tf_op jit(solution)/shard_map/ppermute | solution.py:58
  23.0 2.1 %collective-permute-start.3 = (f32[64,512]{1,0:T(8,128)S(1)}, f32[64,512]{1,0:T(8,128)S(1)}, u32[]{:S(2)}, u32[]{:S(2)}) collective-permute-start(f32[64,512]{1,0:T(8,128)S(1)} %slice_add_fusion.1), channel_id=1, source_target_pairs={{0,8},{1,9},{2,10},{3,11},{4,12},{5,13},{6,14},{7,15},{8,0},{9,1},... | collective-permute-start | bytes 393224 | tf_op jit(solution)/shard_map/ppermute | solution.py:58
  25.1 2.9 %collective-permute-done.3 = f32[64,512]{1,0:T(8,128)S(1)} collective-permute-done((f32[64,512]{1,0:T(8,128)S(1)}, f32[64,512]{1,0:T(8,128)S(1)}, u32[]{:S(2)}, u32[]{:S(2)}) %collective-permute-start.3) | collective-permute-done | bytes 131104 | tf_op jit(solution)/shard_map/ppermute | solution.py:58
  28.1 3.6 %collective-permute-start.4 = (f32[64,512]{1,0:T(8,128)S(1)}, f32[64,512]{1,0:T(8,128)S(1)}, u32[]{:S(2)}, u32[]{:S(2)}) collective-permute-start(f32[64,512]{1,0:T(8,128)S(1)} %add.84), channel_id=1, source_target_pairs={{0,16},{1,17},{2,18},{3,19},{4,20},{5,21},{6,22},{7,23},{8,24},{9,... | collective-permute-start | bytes 393224 | tf_op jit(solution)/shard_map/ppermute | solution.py:58
  31.6 4.4 %collective-permute-done.4 = f32[64,512]{1,0:T(8,128)S(1)} collective-permute-done((f32[64,512]{1,0:T(8,128)S(1)}, f32[64,512]{1,0:T(8,128)S(1)}, u32[]{:S(2)}, u32[]{:S(2)}) %collective-permute-start.4) | collective-permute-done | bytes 131104 | tf_op jit(solution)/shard_map/ppermute | solution.py:58
  36.0 1.6 %collective-permute-start.5 = (f32[64,512]{1,0:T(8,128)S(1)}, f32[64,512]{1,0:T(8,128)S(1)}, u32[]{:S(2)}, u32[]{:S(2)}) collective-permute-start(f32[64,512]{1,0:T(8,128)S(1)} %add.85), channel_id=1, source_target_pairs={{0,2},{1,5},{2,0},{3,7},{4,6},{5,1},{6,4},{7,3},{8,10},{9,13},{10,... | collective-permute-start | bytes 393224 | tf_op jit(solution)/shard_map/ppermute | solution.py:58
  37.6 4.1 %collective-permute-done.5 = f32[64,512]{1,0:T(8,128)S(1)} collective-permute-done((f32[64,512]{1,0:T(8,128)S(1)}, f32[64,512]{1,0:T(8,128)S(1)}, u32[]{:S(2)}, u32[]{:S(2)}) %collective-permute-start.5) | collective-permute-done | bytes 131104 | tf_op jit(solution)/shard_map/ppermute | solution.py:58
  41.7 1.7 %collective-permute-start.6 = (f32[128,512]{1,0:T(8,128)S(1)}, f32[128,512]{1,0:T(8,128)S(1)}, u32[]{:S(2)}, u32[]{:S(2)}) collective-permute-start(f32[128,512]{1,0:T(8,128)S(1)} %pad_maximum_fusion.2), channel_id=1, source_target_pairs={{0,4},{1,3},{2,6},{3,1},{4,0},{5,7},{6,2},{7,5},{8,12},{9,11},{10,... | collective-permute-start | bytes 786440 | tf_op jit(solution)/shard_map/ppermute | solution.py:58
  43.3 4.8 %collective-permute-done.6 = f32[128,512]{1,0:T(8,128)S(1)} collective-permute-done((f32[128,512]{1,0:T(8,128)S(1)}, f32[128,512]{1,0:T(8,128)S(1)}, u32[]{:S(2)}, u32[]{:S(2)}) %collective-permute-start.6) | collective-permute-done | bytes 262176 | tf_op jit(solution)/shard_map/ppermute | solution.py:58
  48.2 0.1 collective-permute-start.7
  48.3 0.0 copy-done.2
  48.3 0.1 copy.9.seeds_ref
  48.4 1.7 %collective-permute-done.7 = f32[256,512]{1,0:T(8,128)S(1)} collective-permute-done((f32[256,512]{1,0:T(8,128)S(1)}, f32[256,512]{1,0:T(8,128)S(1)}, u32[]{:S(2)}, u32[]{:S(2)}) %collective-permute-start.7) | collective-permute-done | bytes 524320 | tf_op jit(solution)/shard_map/ppermute | solution.py:58
  50.2 0.1 pad_maximum_fusion.white_ref
  50.2 29.9 %iterate.1 = (f32[512,512]{1,0:T(8,128)S(1)}, f32[512,1]{1,0:T(8,128)S(1)}) custom-call(s32[1,1,512]{2,1,0:T(1,128)S(1)} %fusion.docs_ref, s32[512,1]{1,0:T(8,128)S(1)} %copy.9.seeds_ref, f32[512,512]{1,0:T(8,128)S(1)} %pad_maximum_fusion.white_ref), custom_call_target="tpu_custom_call" | custom-call | tf_op jit(solution)/shard_map/iterate/pallas_call | solution.py:170
  80.2 0.8 %copy.10 = f32[128,512]{1,0:T(8,128)} copy(f32[128,512]{0,1:T(8,128)S(1)} %multiply_bitcast_fusion) | data formatting | bytes 524288
  81.1 0.7 reduce
  (10 shorter events, 0.2 us)
Async XLA Ops:
  1.4 2.2 %copy-start = (bf16[4096,512]{1,0:T(8,128)(2,1)S(1)}, bf16[4096,512]{1,0:T(8,128)(2,1)}, u32[]{:S(2)}) copy-start(bf16[4096,512]{1,0:T(8,128)(2,1)} %table.1) | copy-start | bytes 12582916
  3.6 1.0 %copy-start.1 = (s32[1,32,2,16,128]{4,3,2,1,0:T(8,128)S(1)}, s32[1,32,2,16,128]{4,3,2,1,0:T(8,128)}, u32[]{:S(2)}) copy-start(s32[1,32,2,16,128]{4,3,2,1,0:T(8,128)} %param.4) | copy-start | bytes 1572868
  4.6 43.6 %copy-start.2 = (s32[512]{0:T(512)S(1)}, s32[512]{0:T(512)}, u32[]{:S(2)}) copy-start(s32[512]{0:T(512)} %param.7) | copy-start | bytes 6148
  8.4 2.1 %collective-permute-start = (f32[256,512]{1,0:T(8,128)S(1)}, f32[256,512]{1,0:T(8,128)S(1)}, u32[]{:S(2)}, u32[]{:S(2)}) collective-permute-start(f32[256,512]{1,0:T(8,128)S(1)} %get-tuple-element.7), channel_id=1, source_target_pairs={{0,1},{1,0},{2,3},{3,2},{4,5},{5,4},{6,7},{7,6},{8,9},{9,8},{10,11... | collective-permute-start | bytes 1572872 | tf_op jit(solution)/shard_map/ppermute | solution.py:58
  10.5 7.3 %collective-permute-start.1 = (f32[128,512]{1,0:T(8,128)S(1)}, f32[128,512]{1,0:T(8,128)S(1)}, u32[]{:S(2)}, u32[]{:S(2)}) collective-permute-start(f32[128,512]{1,0:T(8,128)S(1)} %slice.17), channel_id=1, source_target_pairs={{0,4},{1,3},{2,6},{3,1},{4,0},{5,7},{6,2},{7,5},{8,12},{9,11},{10,... | collective-permute-start | bytes 786440 | tf_op jit(solution)/shard_map/ppermute | solution.py:58
  17.9 5.1 %collective-permute-start.2 = (f32[64,512]{1,0:T(8,128)S(1)}, f32[64,512]{1,0:T(8,128)S(1)}, u32[]{:S(2)}, u32[]{:S(2)}) collective-permute-start(f32[64,512]{1,0:T(8,128)S(1)} %slice.19), channel_id=1, source_target_pairs={{0,2},{1,5},{2,0},{3,7},{4,6},{5,1},{6,4},{7,3},{8,10},{9,13},{10,... | collective-permute-start | bytes 393224 | tf_op jit(solution)/shard_map/ppermute | solution.py:58
  23.0 5.1 %collective-permute-start.3 = (f32[64,512]{1,0:T(8,128)S(1)}, f32[64,512]{1,0:T(8,128)S(1)}, u32[]{:S(2)}, u32[]{:S(2)}) collective-permute-start(f32[64,512]{1,0:T(8,128)S(1)} %slice_add_fusion.1), channel_id=1, source_target_pairs={{0,8},{1,9},{2,10},{3,11},{4,12},{5,13},{6,14},{7,15},{8,0},{9,1},... | collective-permute-start | bytes 393224 | tf_op jit(solution)/shard_map/ppermute | solution.py:58
  28.1 7.9 %collective-permute-start.4 = (f32[64,512]{1,0:T(8,128)S(1)}, f32[64,512]{1,0:T(8,128)S(1)}, u32[]{:S(2)}, u32[]{:S(2)}) collective-permute-start(f32[64,512]{1,0:T(8,128)S(1)} %add.84), channel_id=1, source_target_pairs={{0,16},{1,17},{2,18},{3,19},{4,20},{5,21},{6,22},{7,23},{8,24},{9,... | collective-permute-start | bytes 393224 | tf_op jit(solution)/shard_map/ppermute | solution.py:58
  36.0 5.7 %collective-permute-start.5 = (f32[64,512]{1,0:T(8,128)S(1)}, f32[64,512]{1,0:T(8,128)S(1)}, u32[]{:S(2)}, u32[]{:S(2)}) collective-permute-start(f32[64,512]{1,0:T(8,128)S(1)} %add.85), channel_id=1, source_target_pairs={{0,2},{1,5},{2,0},{3,7},{4,6},{5,1},{6,4},{7,3},{8,10},{9,13},{10,... | collective-permute-start | bytes 393224 | tf_op jit(solution)/shard_map/ppermute | solution.py:58
  41.7 6.4 %collective-permute-start.6 = (f32[128,512]{1,0:T(8,128)S(1)}, f32[128,512]{1,0:T(8,128)S(1)}, u32[]{:S(2)}, u32[]{:S(2)}) collective-permute-start(f32[128,512]{1,0:T(8,128)S(1)} %pad_maximum_fusion.2), channel_id=1, source_target_pairs={{0,4},{1,3},{2,6},{3,1},{4,0},{5,7},{6,2},{7,5},{8,12},{9,11},{10,... | collective-permute-start | bytes 786440 | tf_op jit(solution)/shard_map/ppermute | solution.py:58
  48.2 2.0 %collective-permute-start.7 = (f32[256,512]{1,0:T(8,128)S(1)}, f32[256,512]{1,0:T(8,128)S(1)}, u32[]{:S(2)}, u32[]{:S(2)}) collective-permute-start(f32[256,512]{1,0:T(8,128)S(1)} %pad_maximum_fusion.1), channel_id=1, source_target_pairs={{0,1},{1,0},{2,3},{3,2},{4,5},{5,4},{6,7},{7,6},{8,9},{9,8},{10,11... | collective-permute-start | bytes 1572872 | tf_op jit(solution)/shard_map/ppermute | solution.py:58

commit v2 on v1

v2 whole, which is shorter than its diff:
```python
import functools
import math

import jax
import jax.numpy as jnp
from jax import lax
from jax.experimental import pallas as pl
from jax.experimental.pallas import tpu as pltpu
from jax.sharding import PartitionSpec as P

ITERS = 2
SWEEPS = 4
SHIFT = 2.0
EPS = 1e-06
AXES = ("doc", "vocab")
F32 = jnp.float32
BF16 = jnp.bfloat16
NN = (((1,), (0,)), ((), ()))
NT = (((1,), (1,)), ((), ()))


def split(value):
    high = value.astype(BF16)
    return high, (value - high.astype(F32)).astype(BF16)


def dot(left, right, dims):
    return lax.dot_general(left, right, dims, preferred_element_type=F32)


def product(left, right, dims):
    high = dot(left[0], right[0], dims)
    return high + (dot(left[0], right[1], dims) + dot(left[1], right[0], dims))


def plan(n_doc, n_vocab):
    n = n_doc * n_vocab
    bits = [1 << b for b in range(n.bit_length() - 1)]
    halving, whole = bits[:-2], bits[-2:]
    pairs = [(b, b) for b in halving]
    if len(halving) >= 3:
        pairs[1], pairs[2] = (halving[2], halving[1]), (halving[1], halving[2])
    return pairs, [(b, b) for b in whole]


def unit_at(place, me, pairs):
    steps = len(pairs)
    top = (place >> (steps - 1)) & 1
    odd = (me & 1) ^ top
    unit = (me & ((1 << steps) - 1)) ^ top
    for s in range(1, steps):
        even_mask, odd_mask = pairs[s]
        mask = even_mask + odd * (odd_mask - even_mask)
        unit = unit ^ (((place >> (steps - 1 - s)) & 1) * mask)
    return unit


def exchange(value, masks, n):
    perm = [(i, i ^ masks[i & 1]) for i in range(n)]
    return lax.ppermute(value, AXES, perm)


def whiten_kernel(pairs, unit_blocks, half_blocks, step_blocks, chains, me_ref, words, tiles_in, table, *rest):
    outs, (dense, tiles, held, tile_sem, sems) = rest[: 2 * chains], rest[2 * chains :]
    steps = half_blocks // step_blocks
    step = pl.program_id(0) if steps > 1 else 0
    me = me_ref[0]
    doc_dev, word_block = tiles.shape[2], tiles.shape[3]
    chain_blocks = unit_blocks // chains
    chunk = held.shape[0] // CHUNKS
    cuts = [slice(k * chunk, (k + 1) * chunk) for k in range(CHUNKS)]
    fetch_tiles = pltpu.make_async_copy(tiles_in, tiles, tile_sem)
    fetches = [pltpu.make_async_copy(table.at[cut], held.at[cut], sems.at[k]) for k, cut in enumerate(cuts)]

    def first(action):
        if steps > 1:
            pl.when(step == 0)(action)
        else:
            action()

    @first
    def _():
        fetch_tiles.start()
        for fetch in fetches[:AHEAD]:
            fetch.start()

    dense[...] = jnp.zeros_like(dense)
    first(fetch_tiles.wait)
    for part in range(2 * chains):
        for inside in range(step_blocks):
            place = step * step_blocks + inside + (part % 2) * half_blocks
            unit = unit_at(place // chain_blocks, me, pairs)
            block = unit * unit_blocks + (part // 2) * chain_blocks + place % chain_blocks
            rows = pl.ds((part * step_blocks + inside) * doc_dev, doc_dev)
            for t in range(tiles.shape[1]):
                columns = pl.ds(pl.multiple_of(words[t, block] * word_block, word_block), word_block)
                dense[rows, columns] = dense[rows, columns] + tiles[block, t].astype(F32).astype(BF16)

    value = None
    for k, cut in enumerate(cuts):
        first(fetches[k].wait)
        if k + AHEAD < CHUNKS:
            first(fetches[k + AHEAD].start)
        term = dot(dense[:, cut], held[cut, :], NN)
        value = term if value is None else value + term
    rows = step_blocks * doc_dev
    for part in range(2 * chains):
        outs[part][...] = value[part * rows : (part + 1) * rows]


def partial_rows(tiles, words, table, me, pairs, chains):
    blocks, _, doc_dev, _ = tiles.shape
    topics = table.shape[1]
    unit_blocks = blocks >> len(pairs)
    half_blocks = blocks // 2 // chains
    step_blocks = math.gcd(half_blocks, 16 // chains)
    steps = half_blocks // step_blocks
    step_rows = step_blocks * doc_dev
    half = jax.ShapeDtypeStruct((half_blocks * doc_dev, topics), F32)
    if steps > 1:
        out = pl.BlockSpec((step_rows, topics), lambda i: (i, 0))
    else:
        out = pl.BlockSpec(memory_space=pltpu.VMEM)
    return pl.pallas_call(
        functools.partial(whiten_kernel, pairs, unit_blocks, half_blocks, step_blocks, chains),
        grid=(steps,) if steps > 1 else (),
        in_specs=[
            pl.BlockSpec(memory_space=pltpu.SMEM),
            pl.BlockSpec(memory_space=pltpu.SMEM),
            pl.BlockSpec(memory_space=pl.ANY),
            pl.BlockSpec(memory_space=pl.ANY),
        ],
        out_specs=[out] * (2 * chains),
        out_shape=[half] * (2 * chains),
        scratch_shapes=[
            pltpu.VMEM((2 * chains * step_rows, table.shape[0]), BF16),
            pltpu.VMEM(tiles.shape, jnp.int32),
            pltpu.VMEM(table.shape, BF16),
            pltpu.SemaphoreType.DMA,
            pltpu.SemaphoreType.DMA((CHUNKS,)),
        ],
        compiler_params=pltpu.CompilerParams(vmem_limit_bytes=VMEM_LIMIT),
        name="whiten",
    )(me, words, tiles, table)


def orthonormal(basis_ref, diff_ref, factor_ref):
    topics = basis_ref.shape[0]
    start = (SHIFT / (SHIFT + 1.0)) ** 2
    basis = split(basis_ref[...])
    row = lax.broadcasted_iota(jnp.int32, (topics, topics), 0)
    column = lax.broadcasted_iota(jnp.int32, (topics, topics), 1)
    diff = jnp.where(row == column, start, 0.0).astype(F32) - product(basis, basis, NT)
    e = 1.0 - start
    q = 1.0 + e / 2
    factor = 0.5 * diff
    for sweep in range(1, SWEEPS):
        low = diff.astype(BF16)
        square = dot(low, low, NN)
        mixed = ((3 + 3 * e) / 4) * diff + 0.25 * square
        diff = ((6 * e + 3 * e * e) / 4) * diff + dot(low, mixed.astype(BF16), NN)
        e = (3 * e * e + e * e * e) / 4
        factor = (1.0 + e / 2) * factor + (0.5 * q) * diff + 0.5 * dot(
            factor.astype(BF16), diff.astype(BF16), NN
        )
        q = q * (1.0 + e / 2)
    basis_ref[...] = q * basis_ref[...] + product(split(factor), basis, NN)


def iterate_kernel(chunk, own_ref, docs_ref, seeds_ref, *rest):
    pieces, (own_out, weights_ref, basis_ref, moment_ref, high_ref, low_ref) = rest[:-6], rest[-6:]
    topics = basis_ref.shape[0]
    docs = high_ref.shape[0]
    chunks = docs // chunk
    first = 0
    for piece in pieces:
        rows = slice(first, first + piece.shape[0])
        first = first + piece.shape[0]
        high, low = split(piece[...])
        high_ref[rows, :] = high
        low_ref[rows, :] = low

    def white(i):
        rows = pl.ds(pl.multiple_of(i * chunk, chunk), chunk)
        return high_ref[rows, :], low_ref[rows, :]

    row = lax.broadcasted_iota(jnp.int32, (topics, topics), 0)
    column = lax.broadcasted_iota(jnp.int32, (topics, topics), 1)
    basis_ref[...] = jnp.where(row == column, 1.0, 0.0).astype(F32)

    def turn(number, carry):
        moment_ref[...] = jnp.zeros_like(moment_ref)

        def add(i, carry):
            high, low = white(i)

            @pl.when(number == 0)
            def _():
                hits = (seeds_ref[...] == docs_ref[i]).astype(F32).astype(BF16)
                moment_ref[...] += dot(hits, high, NN) + dot(hits, low, NN)

            @pl.when(number > 0)
            def _():
                value = product(split(basis_ref[...]), (high, low), NT)
                moment_ref[...] += product(split(value * value), (high, low), NN)

            return carry

        lax.fori_loop(0, chunks, add, 0)
        moment = moment_ref[...]
        scale = topics * jnp.sqrt(jnp.mean(moment * moment) + EPS)
        basis_ref[...] = moment * (1.0 / ((SHIFT + 1.0) * scale)) + (SHIFT / (SHIFT + 1.0)) * basis_ref[...]
        orthonormal(basis_ref, None, None)
        return carry

    lax.fori_loop(0, ITERS + 1, turn, 0)
    parts = split(basis_ref[...])
    total = jnp.zeros((1, topics), F32)
    for i in range(chunks):
        value = product(white(i), parts, NT)
        total += jnp.sum(value * value * value, axis=0, keepdims=True)
    weights_ref[...] = total / docs
    moment_ref[...] = basis_ref[...].T * math.sqrt(topics)
    own_rows = own_out.shape[0]
    own_out[...] = moment_ref[pl.ds(pl.multiple_of(own_ref[0] * own_rows, own_rows), own_rows), :]


def iterate(pieces, docs_row, seeds, own, own_rows):
    docs = docs_row.shape[0]
    topics = seeds.shape[0]
    chunk = math.gcd(docs, 512)
    vmem = pl.BlockSpec(memory_space=pltpu.VMEM)
    return pl.pallas_call(
        functools.partial(iterate_kernel, chunk),
        in_specs=[pl.BlockSpec(memory_space=pltpu.SMEM)] + [vmem] * (2 + len(pieces)),
        out_specs=[vmem] * 2,
        out_shape=[
            jax.ShapeDtypeStruct((own_rows, topics), F32),
            jax.ShapeDtypeStruct((1, topics), F32),
        ],
        scratch_shapes=[
            pltpu.VMEM((topics, topics), F32),
            pltpu.VMEM((topics, topics), F32),
            pltpu.VMEM((docs, topics), BF16),
            pltpu.VMEM((docs, topics), BF16),
        ],
        compiler_params=pltpu.CompilerParams(vmem_limit_bytes=40 << 20),
        name="iterate",
    )(own, docs_row.reshape(docs // chunk, 1, chunk), seeds.reshape(topics, 1), *pieces)


CHAINS = 2
VMEM_LIMIT = 53 << 20
CHUNKS = 4
AHEAD = 2
SWAP = True


def per_device(n_doc, n_vocab, count_tiles, tile_words, whitening, seeds):
    n = n_doc * n_vocab
    pairs, whole = plan(n_doc, n_vocab)
    me = lax.axis_index(AXES).astype(jnp.int32)
    halves = partial_rows(count_tiles[0], tile_words[0].T, whitening, me.reshape(1), pairs, CHAINS)
    rows, topics = halves[0].shape[0] * 2, whitening.shape[1]
    docs = rows * CHAINS
    values = [keep + exchange(send, pairs[0], n) for keep, send in zip(halves[::2], halves[1::2])]
    half = rows // 2
    for masks in pairs[1:]:
        half = half // 2
        values = [v[:half] + exchange(v[half:], masks, n) for v in values]
    for s in range(len(whole)):
        values = [v + exchange(v, whole[s ^ (c & 1) if SWAP else s], n) for c, v in enumerate(values)]
    for masks in reversed(pairs[1:]):
        values = [jnp.concatenate([v, exchange(v, masks, n)]) for v in values]
    pieces = []
    for v in values:
        pieces += [v, exchange(v, pairs[0], n)]
    place = jnp.arange(docs, dtype=jnp.int32)
    chain_rows = (docs >> len(pairs)) // CHAINS
    unit = unit_at(place % rows // chain_rows, me, pairs)
    docs_row = unit * (chain_rows * CHAINS) + place // rows * chain_rows + place % chain_rows
    own = lax.axis_index("vocab").astype(jnp.int32).reshape(1)
    directions, weights = iterate(pieces, docs_row, seeds, own, topics // n_vocab)
    return directions, weights.reshape(topics)


def solution(mesh):
    in_specs = (
        P(("doc", "vocab"), None, None, None, None),
        P(("doc", "vocab"), None, None),
        P(("doc", "vocab"), None),
        P(),
    )
    out_specs = (P("vocab", None), P())
    return jax.shard_map(
        functools.partial(per_device, mesh.shape["doc"], mesh.shape["vocab"]),
        mesh=mesh,
        in_specs=in_specs,
        out_specs=out_specs,
        check_vma=False,
    )
```

time: 82 us -> 66.4 us (0.81)
  waiting for transfers between devices: 26.7 us -> 11.9 us
  starting transfers between devices: 14.6 us -> 23.8 us
  Pallas kernels: 33.7 us -> 28.6 us
  local copies, waits for them, and re-layouts: 5 us -> 0.85 us
  other arithmetic: 1.09 us -> 0.26 us
    ppermute x8 -> x16, waiting for transfers between devices: 26.7 us -> 11.9 us  [exchange(): return lax.ppermute(value, AXES, perm)]
    ppermute x8 -> x16, starting transfers between devices: 14.6 us -> 23.8 us  [exchange(): return lax.ppermute(value, AXES, perm)]
    pallas_call x1, Pallas kernels: 29.9 us -> 23.1 us  [iterate(): pl.pallas_call(functools.partial(iterate_kernel, chunk), in_specs=[pl.Blo...]
    unnamed x7 -> x4, local copies, waits for them, and re-layouts: 4.07 us -> 0.68 us
    pallas_call x1, Pallas kernels: 3.74 us -> 5.53 us  [partial_rows(): pl.pallas_call(functools.partial(whiten_kernel, pairs, unit_blocks, half_...]
  transfers between devices with their start and end apart: 8 -> 16, of which waited for: 8 -> 11; matrix products, arithmetic and copies ran while one was open for 0% -> 1% of each run, Pallas kernels for 0% -> 0%
where the time goes in v2:
time: 66.4 us; the launch traced here: 66.2 us
  Pallas kernels  28.6 us (43%)
  starting transfers between devices  23.8 us (36%)
  waiting for transfers between devices  11.9 us (18%)
  local copies, waits for them, and re-layouts  0.85 us (1%)
  between operations  0.79 us (1%)
    ppermute x16, starting transfers between devices, exchange(): return lax.ppermute(value, AXES, perm)  23.8 us
    pallas_call x1, Pallas kernels, iterate(): pl.pallas_call(functools.partial(iterate_kernel, chunk), in_specs=[pl.Blo...  23.1 us
    ppermute x16, waiting for transfers between devices, exchange(): return lax.ppermute(value, AXES, perm)  11.9 us
    pallas_call x1, Pallas kernels, partial_rows(): pl.pallas_call(functools.partial(whiten_kernel, pairs, unit_blocks, half_...  5.53 us
  transfers between devices with their start and end apart: 16, of which 11 were waited for; matrix products, arithmetic and copies ran while one was open for 1% of the time, Pallas kernels for 0%

profile of v2, /device:TPU:0, one launch (start us, length us, event | category | flops | bytes accessed | tf_op | source)
XLA Modules:
  0.0 66.2 jit_solution(5059643562725532011)
XLA Ops:
  0.6 0.7 %copy-done = s32[1,32,2]{1,2,0:T(2,128)S(1)} copy-done((s32[1,32,2]{1,2,0:T(2,128)S(1)}, s32[1,32,2]{1,2,0:T(2,128)}, u32[]{:S(2)}) %copy-start) | copy-done | bytes 280
  1.3 5.5 %whiten.1 = (f32[128,512]{1,0:T(8,128)S(1)}, f32[128,512]{1,0:T(8,128)S(1)}, f32[128,512]{1,0:T(8,128)S(1)}, f32[128,512]{1,0:T(8,128)}) custom-call(s32[1]{0:T(128)} %bitcast.2.me_ref, s32[2,32]{1,0:T(2,128)S(1)} %bitcast.8, s32[32,2,16,128]{3,2,1,0:T(8,128)} %bitcast.9, bf16[4096,512]{1,0:T(8,128)(2,1)} %table.1), custom_call_target="tpu_custom_call" | custom-call | tf_op jit(solution)/shard_map/whiten/pallas_call | solution.py:124
  6.9 0.5 collective-permute-start.8
  7.4 0.1 collective-permute-start
  7.5 1.3 %collective-permute-done.8 = f32[128,512]{1,0:T(8,128)S(1)} collective-permute-done((f32[128,512]{1,0:T(8,128)}, f32[128,512]{1,0:T(8,128)S(1)}, u32[]{:S(2)}, u32[]{:S(2)}) %collective-permute-start.8) | collective-permute-done | bytes 262176 | tf_op jit(solution)/shard_map/ppermute | solution.py:60
  8.8 2.9 %collective-permute-start.9 = (f32[64,512]{1,0:T(8,128)S(1)}, f32[64,512]{1,0:T(8,128)S(1)}, u32[]{:S(2)}, u32[]{:S(2)}) collective-permute-start(f32[64,512]{1,0:T(8,128)S(1)} %slice.37), channel_id=1, source_target_pairs={{0,4},{1,3},{2,6},{3,1},{4,0},{5,7},{6,2},{7,5},{8,12},{9,11},{10,... | collective-permute-start | bytes 393224 | tf_op jit(solution)/shard_map/ppermute | solution.py:60
  11.8 0.1 collective-permute-start.1
  11.9 2.8 %collective-permute-done.9 = f32[64,512]{1,0:T(8,128)S(1)} collective-permute-done((f32[64,512]{1,0:T(8,128)S(1)}, f32[64,512]{1,0:T(8,128)S(1)}, u32[]{:S(2)}, u32[]{:S(2)}) %collective-permute-start.9) | collective-permute-done | bytes 131104 | tf_op jit(solution)/shard_map/ppermute | solution.py:60
  14.7 2.1 %collective-permute-start.10 = (f32[32,512]{1,0:T(8,128)S(1)}, f32[32,512]{1,0:T(8,128)S(1)}, u32[]{:S(2)}, u32[]{:S(2)}) collective-permute-start(f32[32,512]{1,0:T(8,128)S(1)} %slice.39), channel_id=1, source_target_pairs={{0,2},{1,5},{2,0},{3,7},{4,6},{5,1},{6,4},{7,3},{8,10},{9,13},{10,... | collective-permute-start | bytes 196616 | tf_op jit(solution)/shard_map/ppermute | solution.py:60
  16.8 0.0 collective-permute-done.1
  16.9 1.6 %collective-permute-start.2 = (f32[32,512]{1,0:T(8,128)S(1)}, f32[32,512]{1,0:T(8,128)S(1)}, u32[]{:S(2)}, u32[]{:S(2)}) collective-permute-start(f32[32,512]{1,0:T(8,128)S(1)} %slice.35), channel_id=1, source_target_pairs={{0,2},{1,5},{2,0},{3,7},{4,6},{5,1},{6,4},{7,3},{8,10},{9,13},{10,... | collective-permute-start | bytes 196616 | tf_op jit(solution)/shard_map/ppermute | solution.py:60
  18.5 0.6 collective-permute-done.10
  19.1 3.2 %collective-permute-start.11 = (f32[32,512]{1,0:T(8,128)S(1)}, f32[32,512]{1,0:T(8,128)S(1)}, u32[]{:S(2)}, u32[]{:S(2)}) collective-permute-start(f32[32,512]{1,0:T(8,128)S(1)} %slice_add_fusion.2), channel_id=1, source_target_pairs={{0,16},{1,17},{2,18},{3,19},{4,20},{5,21},{6,22},{7,23},{8,24},{9,... | collective-permute-start | bytes 196616 | tf_op jit(solution)/shard_map/ppermute | solution.py:60
  22.3 1.6 %collective-permute-start.3 = (f32[32,512]{1,0:T(8,128)S(1)}, f32[32,512]{1,0:T(8,128)S(1)}, u32[]{:S(2)}, u32[]{:S(2)}) collective-permute-start(f32[32,512]{1,0:T(8,128)S(1)} %slice_add_fusion.3), channel_id=1, source_target_pairs={{0,8},{1,9},{2,10},{3,11},{4,12},{5,13},{6,14},{7,15},{8,0},{9,1},... | collective-permute-start | bytes 196616 | tf_op jit(solution)/shard_map/ppermute | solution.py:60
  23.9 0.6 collective-permute-done.11
  24.5 2.0 %collective-permute-start.12 = (f32[32,512]{1,0:T(8,128)S(1)}, f32[32,512]{1,0:T(8,128)S(1)}, u32[]{:S(2)}, u32[]{:S(2)}) collective-permute-start(f32[32,512]{1,0:T(8,128)S(1)} %add.138), channel_id=1, source_target_pairs={{0,8},{1,9},{2,10},{3,11},{4,12},{5,13},{6,14},{7,15},{8,0},{9,1},... | collective-permute-start | bytes 196616 | tf_op jit(solution)/shard_map/ppermute | solution.py:60
  26.5 0.1 collective-permute-done.3
  26.6 3.2 %collective-permute-start.4 = (f32[32,512]{1,0:T(8,128)S(1)}, f32[32,512]{1,0:T(8,128)S(1)}, u32[]{:S(2)}, u32[]{:S(2)}) collective-permute-start(f32[32,512]{1,0:T(8,128)S(1)} %add.133), channel_id=1, source_target_pairs={{0,16},{1,17},{2,18},{3,19},{4,20},{5,21},{6,22},{7,23},{8,24},{9,... | collective-permute-start | bytes 196616 | tf_op jit(solution)/shard_map/ppermute | solution.py:60
  29.9 1.6 %collective-permute-start.13 = (f32[32,512]{1,0:T(8,128)S(1)}, f32[32,512]{1,0:T(8,128)S(1)}, u32[]{:S(2)}, u32[]{:S(2)}) collective-permute-start(f32[32,512]{1,0:T(8,128)S(1)} %add.139), channel_id=1, source_target_pairs={{0,2},{1,5},{2,0},{3,7},{4,6},{5,1},{6,4},{7,3},{8,10},{9,13},{10,... | collective-permute-start | bytes 196616 | tf_op jit(solution)/shard_map/ppermute | solution.py:60
  31.4 0.6 collective-permute-done.4
  32.1 1.6 %collective-permute-start.5 = (f32[32,512]{1,0:T(8,128)S(1)}, f32[32,512]{1,0:T(8,128)S(1)}, u32[]{:S(2)}, u32[]{:S(2)}) collective-permute-start(f32[32,512]{1,0:T(8,128)S(1)} %add.134), channel_id=1, source_target_pairs={{0,2},{1,5},{2,0},{3,7},{4,6},{5,1},{6,4},{7,3},{8,10},{9,13},{10,... | collective-permute-start | bytes 196616 | tf_op jit(solution)/shard_map/ppermute | solution.py:60
  33.7 1.0 %collective-permute-done.13 = f32[32,512]{1,0:T(8,128)S(1)} collective-permute-done((f32[32,512]{1,0:T(8,128)S(1)}, f32[32,512]{1,0:T(8,128)S(1)}, u32[]{:S(2)}, u32[]{:S(2)}) %collective-permute-start.13) | collective-permute-done | bytes 65568 | tf_op jit(solution)/shard_map/ppermute | solution.py:60
  34.7 1.6 %collective-permute-start.14 = (f32[64,512]{1,0:T(8,128)S(1)}, f32[64,512]{1,0:T(8,128)S(1)}, u32[]{:S(2)}, u32[]{:S(2)}) collective-permute-start(f32[64,512]{1,0:T(8,128)S(1)} %pad_maximum_fusion.3), channel_id=1, source_target_pairs={{0,4},{1,3},{2,6},{3,1},{4,0},{5,7},{6,2},{7,5},{8,12},{9,11},{10,... | collective-permute-start | bytes 393224 | tf_op jit(solution)/shard_map/ppermute | solution.py:60
  36.2 0.2 collective-permute-done.5
  36.5 1.6 %collective-permute-start.6 = (f32[64,512]{1,0:T(8,128)S(1)}, f32[64,512]{1,0:T(8,128)S(1)}, u32[]{:S(2)}, u32[]{:S(2)}) collective-permute-start(f32[64,512]{1,0:T(8,128)S(1)} %pad_maximum_fusion.2), channel_id=1, source_target_pairs={{0,4},{1,3},{2,6},{3,1},{4,0},{5,7},{6,2},{7,5},{8,12},{9,11},{10,... | collective-permute-start | bytes 393224 | tf_op jit(solution)/shard_map/ppermute | solution.py:60
  38.0 1.7 %collective-permute-done.14 = f32[64,512]{1,0:T(8,128)S(1)} collective-permute-done((f32[64,512]{1,0:T(8,128)S(1)}, f32[64,512]{1,0:T(8,128)S(1)}, u32[]{:S(2)}, u32[]{:S(2)}) %collective-permute-start.14) | collective-permute-done | bytes 131104 | tf_op jit(solution)/shard_map/ppermute | solution.py:60
  39.7 0.1 collective-permute-start.15
  39.8 1.7 %collective-permute-done.6 = f32[64,512]{1,0:T(8,128)S(1)} collective-permute-done((f32[64,512]{1,0:T(8,128)S(1)}, f32[64,512]{1,0:T(8,128)S(1)}, u32[]{:S(2)}, u32[]{:S(2)}) %collective-permute-start.6) | collective-permute-done | bytes 131104 | tf_op jit(solution)/shard_map/ppermute | solution.py:60
  41.5 0.1 collective-permute-start.7
  41.6 0.1 copy.6.seeds_ref
  41.8 1.3 %collective-permute-done.7.rest_1_ = f32[128,512]{1,0:T(8,128)S(1)} collective-permute-done((f32[128,512]{1,0:T(8,128)S(1)}, f32[128,512]{1,0:T(8,128)S(1)}, u32[]{:S(2)}, u32[]{:S(2)}) %collective-permute-start.7) | collective-permute-done | bytes 262176 | tf_op jit(solution)/shard_map/ppermute | solution.py:60
  43.1 23.1 %iterate.1 = (f32[128,512]{1,0:T(8,128)}, f32[1,512]{1,0:T(1,128)}) custom-call(s32[1]{0:T(128)} %bitcast.own_ref, s32[1,1,512]{2,1,0:T(1,128)S(1)} %fusion.docs_ref, s32[512,1]{1,0:T(8,128)S(1)} %copy.6.seeds_ref, f32[128,512]{1,0:T(8,128)S(1)} %pad_maximum_fusion.rest_0_, f32[128,512]{1,0:T(8,128)S(1)} %collective-permute-done.7.rest_1_, ...), custom_call_target="tpu_custom_call" | custom-call | tf_op jit(solution)/shard_map/iterate/pallas_call | solution.py:233
  (26 shorter events, 0.3 us)
Async XLA Ops:
  0.6 0.7 %copy-start = (s32[1,32,2]{1,2,0:T(2,128)S(1)}, s32[1,32,2]{1,2,0:T(2,128)}, u32[]{:S(2)}) copy-start(s32[1,32,2]{1,2,0:T(2,128)} %param.5) | copy-start | bytes 772
  1.3 40.3 %copy-start.1 = (s32[512]{0:T(512)S(1)}, s32[512]{0:T(512)}, u32[]{:S(2)}) copy-start(s32[512]{0:T(512)} %param.7) | copy-start | bytes 6148
  6.9 1.9 %collective-permute-start.8 = (f32[128,512]{1,0:T(8,128)}, f32[128,512]{1,0:T(8,128)S(1)}, u32[]{:S(2)}, u32[]{:S(2)}) collective-permute-start(f32[128,512]{1,0:T(8,128)} %get-tuple-element.11), channel_id=1, source_target_pairs={{0,1},{1,0},{2,3},{3,2},{4,5},{5,4},{6,7},{7,6},{8,9},{9,8},{10,11... | collective-permute-start | bytes 786440 | tf_op jit(solution)/shard_map/ppermute | solution.py:60
  7.4 4.4 %collective-permute-start = (f32[128,512]{1,0:T(8,128)S(1)}, f32[128,512]{1,0:T(8,128)S(1)}, u32[]{:S(2)}, u32[]{:S(2)}) collective-permute-start(f32[128,512]{1,0:T(8,128)S(1)} %get-tuple-element.9), channel_id=1, source_target_pairs={{0,1},{1,0},{2,3},{3,2},{4,5},{5,4},{6,7},{7,6},{8,9},{9,8},{10,11... | collective-permute-start | bytes 786440 | tf_op jit(solution)/shard_map/ppermute | solution.py:60
  8.8 5.9 %collective-permute-start.9 = (f32[64,512]{1,0:T(8,128)S(1)}, f32[64,512]{1,0:T(8,128)S(1)}, u32[]{:S(2)}, u32[]{:S(2)}) collective-permute-start(f32[64,512]{1,0:T(8,128)S(1)} %slice.37), channel_id=1, source_target_pairs={{0,4},{1,3},{2,6},{3,1},{4,0},{5,7},{6,2},{7,5},{8,12},{9,11},{10,... | collective-permute-start | bytes 393224 | tf_op jit(solution)/shard_map/ppermute | solution.py:60
  11.8 5.0 %collective-permute-start.1 = (f32[64,512]{1,0:T(8,128)S(1)}, f32[64,512]{1,0:T(8,128)S(1)}, u32[]{:S(2)}, u32[]{:S(2)}) collective-permute-start(f32[64,512]{1,0:T(8,128)S(1)} %slice.33), channel_id=1, source_target_pairs={{0,4},{1,3},{2,6},{3,1},{4,0},{5,7},{6,2},{7,5},{8,12},{9,11},{10,... | collective-permute-start | bytes 393224 | tf_op jit(solution)/shard_map/ppermute | solution.py:60
  14.7 4.4 %collective-permute-start.10 = (f32[32,512]{1,0:T(8,128)S(1)}, f32[32,512]{1,0:T(8,128)S(1)}, u32[]{:S(2)}, u32[]{:S(2)}) collective-permute-start(f32[32,512]{1,0:T(8,128)S(1)} %slice.39), channel_id=1, source_target_pairs={{0,2},{1,5},{2,0},{3,7},{4,6},{5,1},{6,4},{7,3},{8,10},{9,13},{10,... | collective-permute-start | bytes 196616 | tf_op jit(solution)/shard_map/ppermute | solution.py:60
  16.9 5.4 %collective-permute-start.2 = (f32[32,512]{1,0:T(8,128)S(1)}, f32[32,512]{1,0:T(8,128)S(1)}, u32[]{:S(2)}, u32[]{:S(2)}) collective-permute-start(f32[32,512]{1,0:T(8,128)S(1)} %slice.35), channel_id=1, source_target_pairs={{0,2},{1,5},{2,0},{3,7},{4,6},{5,1},{6,4},{7,3},{8,10},{9,13},{10,... | collective-permute-start | bytes 196616 | tf_op jit(solution)/shard_map/ppermute | solution.py:60
  19.1 5.4 %collective-permute-start.11 = (f32[32,512]{1,0:T(8,128)S(1)}, f32[32,512]{1,0:T(8,128)S(1)}, u32[]{:S(2)}, u32[]{:S(2)}) collective-permute-start(f32[32,512]{1,0:T(8,128)S(1)} %slice_add_fusion.2), channel_id=1, source_target_pairs={{0,16},{1,17},{2,18},{3,19},{4,20},{5,21},{6,22},{7,23},{8,24},{9,... | collective-permute-start | bytes 196616 | tf_op jit(solution)/shard_map/ppermute | solution.py:60
  22.3 4.3 %collective-permute-start.3 = (f32[32,512]{1,0:T(8,128)S(1)}, f32[32,512]{1,0:T(8,128)S(1)}, u32[]{:S(2)}, u32[]{:S(2)}) collective-permute-start(f32[32,512]{1,0:T(8,128)S(1)} %slice_add_fusion.3), channel_id=1, source_target_pairs={{0,8},{1,9},{2,10},{3,11},{4,12},{5,13},{6,14},{7,15},{8,0},{9,1},... | collective-permute-start | bytes 196616 | tf_op jit(solution)/shard_map/ppermute | solution.py:60
  24.5 5.3 %collective-permute-start.12 = (f32[32,512]{1,0:T(8,128)S(1)}, f32[32,512]{1,0:T(8,128)S(1)}, u32[]{:S(2)}, u32[]{:S(2)}) collective-permute-start(f32[32,512]{1,0:T(8,128)S(1)} %add.138), channel_id=1, source_target_pairs={{0,8},{1,9},{2,10},{3,11},{4,12},{5,13},{6,14},{7,15},{8,0},{9,1},... | collective-permute-start | bytes 196616 | tf_op jit(solution)/shard_map/ppermute | solution.py:60
  26.6 5.5 %collective-permute-start.4 = (f32[32,512]{1,0:T(8,128)S(1)}, f32[32,512]{1,0:T(8,128)S(1)}, u32[]{:S(2)}, u32[]{:S(2)}) collective-permute-start(f32[32,512]{1,0:T(8,128)S(1)} %add.133), channel_id=1, source_target_pairs={{0,16},{1,17},{2,18},{3,19},{4,20},{5,21},{6,22},{7,23},{8,24},{9,... | collective-permute-start | bytes 196616 | tf_op jit(solution)/shard_map/ppermute | solution.py:60
  29.9 4.8 %collective-permute-start.13 = (f32[32,512]{1,0:T(8,128)S(1)}, f32[32,512]{1,0:T(8,128)S(1)}, u32[]{:S(2)}, u32[]{:S(2)}) collective-permute-start(f32[32,512]{1,0:T(8,128)S(1)} %add.139), channel_id=1, source_target_pairs={{0,2},{1,5},{2,0},{3,7},{4,6},{5,1},{6,4},{7,3},{8,10},{9,13},{10,... | collective-permute-start | bytes 196616 | tf_op jit(solution)/shard_map/ppermute | solution.py:60
  32.1 4.3 %collective-permute-start.5 = (f32[32,512]{1,0:T(8,128)S(1)}, f32[32,512]{1,0:T(8,128)S(1)}, u32[]{:S(2)}, u32[]{:S(2)}) collective-permute-start(f32[32,512]{1,0:T(8,128)S(1)} %add.134), channel_id=1, source_target_pairs={{0,2},{1,5},{2,0},{3,7},{4,6},{5,1},{6,4},{7,3},{8,10},{9,13},{10,... | collective-permute-start | bytes 196616 | tf_op jit(solution)/shard_map/ppermute | solution.py:60
  34.7 5.0 %collective-permute-start.14 = (f32[64,512]{1,0:T(8,128)S(1)}, f32[64,512]{1,0:T(8,128)S(1)}, u32[]{:S(2)}, u32[]{:S(2)}) collective-permute-start(f32[64,512]{1,0:T(8,128)S(1)} %pad_maximum_fusion.3), channel_id=1, source_target_pairs={{0,4},{1,3},{2,6},{3,1},{4,0},{5,7},{6,2},{7,5},{8,12},{9,11},{10,... | collective-permute-start | bytes 393224 | tf_op jit(solution)/shard_map/ppermute | solution.py:60
  36.5 5.0 %collective-permute-start.6 = (f32[64,512]{1,0:T(8,128)S(1)}, f32[64,512]{1,0:T(8,128)S(1)}, u32[]{:S(2)}, u32[]{:S(2)}) collective-permute-start(f32[64,512]{1,0:T(8,128)S(1)} %pad_maximum_fusion.2), channel_id=1, source_target_pairs={{0,4},{1,3},{2,6},{3,1},{4,0},{5,7},{6,2},{7,5},{8,12},{9,11},{10,... | collective-permute-start | bytes 393224 | tf_op jit(solution)/shard_map/ppermute | solution.py:60
  39.7 2.1 %collective-permute-start.15 = (f32[128,512]{1,0:T(8,128)S(1)}, f32[128,512]{1,0:T(8,128)S(1)}, u32[]{:S(2)}, u32[]{:S(2)}) collective-permute-start(f32[128,512]{1,0:T(8,128)S(1)} %pad_maximum_fusion.1.rest_2_), channel_id=1, source_target_pairs={{0,1},{1,0},{2,3},{3,2},{4,5},{5,4},{6,7},{7,6},{8,9},{9,8},{10,11... | collective-permute-start | bytes 786440 | tf_op jit(solution)/shard_map/ppermute | solution.py:60
  41.5 1.6 %collective-permute-start.7 = (f32[128,512]{1,0:T(8,128)S(1)}, f32[128,512]{1,0:T(8,128)S(1)}, u32[]{:S(2)}, u32[]{:S(2)}) collective-permute-start(f32[128,512]{1,0:T(8,128)S(1)} %pad_maximum_fusion.rest_0_), channel_id=1, source_target_pairs={{0,1},{1,0},{2,3},{3,2},{4,5},{5,4},{6,7},{7,6},{8,9},{9,8},{10,11... | collective-permute-start | bytes 786440 | tf_op jit(solution)/shard_map/ppermute | solution.py:60

commit v3 on v2

v3 whole, which is shorter than its diff:
```python
import functools
import math

import jax
import jax.numpy as jnp
from jax import lax
from jax.experimental import pallas as pl
from jax.experimental.pallas import tpu as pltpu
from jax.sharding import PartitionSpec as P

ITERS = 2
SWEEPS = 4
SHIFT = 2.0
EPS = 1e-06
AXES = ("doc", "vocab")
F32 = jnp.float32
BF16 = jnp.bfloat16
NN = (((1,), (0,)), ((), ()))
NT = (((1,), (1,)), ((), ()))


def split(value):
    high = value.astype(BF16)
    return high, (value - high.astype(F32)).astype(BF16)


def dot(left, right, dims):
    return lax.dot_general(left, right, dims, preferred_element_type=F32)


def product(left, right, dims):
    high = dot(left[0], right[0], dims)
    return high + (dot(left[0], right[1], dims) + dot(left[1], right[0], dims))


def plan(n_doc, n_vocab):
    n = n_doc * n_vocab
    bits = [1 << b for b in range(n.bit_length() - 1)]
    halving, whole = bits[:-2], bits[-2:]
    pairs = [(b, b) for b in halving]
    if len(halving) >= 3:
        pairs[1], pairs[2] = (halving[2], halving[1]), (halving[1], halving[2])
    return pairs, [(b, b) for b in whole]


def unit_at(place, me, pairs):
    steps = len(pairs)
    top = (place >> (steps - 1)) & 1
    odd = (me & 1) ^ top
    unit = (me & ((1 << steps) - 1)) ^ top
    for s in range(1, steps):
        even_mask, odd_mask = pairs[s]
        mask = even_mask + odd * (odd_mask - even_mask)
        unit = unit ^ (((place >> (steps - 1 - s)) & 1) * mask)
    return unit


def position():
    return lax.axis_index("doc") * lax.axis_size("vocab") + lax.axis_index("vocab")


def exchange(value, masks, n):
    perm = [(i, i ^ masks[i & 1]) for i in range(n)]
    return lax.ppermute(value, AXES, perm)


def whiten_kernel(pairs, unit_blocks, half_blocks, step_blocks, chains, words_in, tiles_in, table, *rest):
    outs, (words, dense, tiles, held, word_sem, tile_sem, sems) = rest[: 2 * chains], rest[2 * chains :]
    steps = half_blocks // step_blocks
    step = pl.program_id(0) if steps > 1 else 0
    me = position()
    doc_dev, word_block = tiles.shape[2], tiles.shape[3]
    chain_blocks = unit_blocks // chains
    chunk = held.shape[0] // CHUNKS
    cuts = [slice(k * chunk, (k + 1) * chunk) for k in range(CHUNKS)]
    fetch_words = pltpu.make_async_copy(words_in, words, word_sem)
    fetch_tiles = pltpu.make_async_copy(tiles_in, tiles, tile_sem)
    fetches = [pltpu.make_async_copy(table.at[cut], held.at[cut], sems.at[k]) for k, cut in enumerate(cuts)]

    def first(action):
        if steps > 1:
            pl.when(step == 0)(action)
        else:
            action()

    @first
    def _():
        fetch_words.start()
        fetch_tiles.start()
        for fetch in fetches[:AHEAD]:
            fetch.start()

    dense[...] = jnp.zeros_like(dense)
    first(fetch_words.wait)
    first(fetch_tiles.wait)
    for part in range(2 * chains):
        for inside in range(step_blocks):
            place = step * step_blocks + inside + (part % 2) * half_blocks
            unit = unit_at(place // chain_blocks, me, pairs)
            block = unit * unit_blocks + (part // 2) * chain_blocks + place % chain_blocks
            rows = pl.ds((part * step_blocks + inside) * doc_dev, doc_dev)
            for t in range(tiles.shape[1]):
                columns = pl.ds(pl.multiple_of(words[t, block] * word_block, word_block), word_block)
                dense[rows, columns] = dense[rows, columns] + tiles[block, t].astype(F32).astype(BF16)

    value = None
    for k, cut in enumerate(cuts):
        first(fetches[k].wait)
        if k + AHEAD < CHUNKS:
            first(fetches[k + AHEAD].start)
        term = dot(dense[:, cut], held[cut, :], NN)
        value = term if value is None else value + term
    rows = step_blocks * doc_dev
    for part in range(2 * chains):
        outs[part][...] = value[part * rows : (part + 1) * rows]


def partial_rows(tiles, words, table, pairs, chains):
    blocks, _, doc_dev, _ = tiles.shape
    topics = table.shape[1]
    unit_blocks = blocks >> len(pairs)
    half_blocks = blocks // 2 // chains
    step_blocks = math.gcd(half_blocks, 16 // chains)
    steps = half_blocks // step_blocks
    step_rows = step_blocks * doc_dev
    half = jax.ShapeDtypeStruct((half_blocks * doc_dev, topics), F32)
    if steps > 1:
        out = pl.BlockSpec((step_rows, topics), lambda i: (i, 0))
    else:
        out = pl.BlockSpec(memory_space=pltpu.VMEM)
    return pl.pallas_call(
        functools.partial(whiten_kernel, pairs, unit_blocks, half_blocks, step_blocks, chains),
        grid=(steps,) if steps > 1 else (),
        in_specs=[
            pl.BlockSpec(memory_space=pl.ANY),
            pl.BlockSpec(memory_space=pl.ANY),
            pl.BlockSpec(memory_space=pl.ANY),
        ],
        out_specs=[out] * (2 * chains),
        out_shape=[half] * (2 * chains),
        scratch_shapes=[
            pltpu.SMEM(words.shape, jnp.int32),
            pltpu.VMEM((2 * chains * step_rows, table.shape[0]), BF16),
            pltpu.VMEM(tiles.shape, jnp.int32),
            pltpu.VMEM(table.shape, BF16),
            pltpu.SemaphoreType.DMA,
            pltpu.SemaphoreType.DMA,
            pltpu.SemaphoreType.DMA((CHUNKS,)),
        ],
        compiler_params=pltpu.CompilerParams(vmem_limit_bytes=VMEM_LIMIT),
        name="whiten",
    )(words, tiles, table)


def series(e):
    return (
        1.0 + e / 2 + 0.375 * e**2 + 0.3125 * e**3 + 0.0625 * e**4,
        0.5 + 0.75 * e + 0.9375 * e**2 + 0.25 * e**3,
        0.375 + 0.9375 * e + 0.375 * e**2,
        0.3125 + 0.25 * e,
        0.0625,
    )


def following(e):
    return (3 * e**2 + e**3) / 4, (6 * e + 3 * e**2) / 4, (3 + 3 * e) / 4, 0.25


def iterate_kernel(chunk, pairs, chains, seeds_ref, *rest):
    refs, pieces = rest[-SCRATCH - 2 :], rest[: -SCRATCH - 2]
    own_out, weights_ref, basis, white_high, white_low, basis_high, basis_low, diff_high, factor_high, square_high = refs
    topics = basis.shape[0]
    docs = white_high.shape[0]
    chunks = docs // chunk
    blocks = [slice(r, r + BLOCK) for r in range(0, topics, BLOCK)]
    each = range(len(blocks))
    first = 0
    for piece in pieces:
        rows = slice(first, first + piece.shape[0])
        first = first + piece.shape[0]
        white_high[rows, :], white_low[rows, :] = split(piece[...])

    def diagonal(rows, value):
        row = lax.broadcasted_iota(jnp.int32, (BLOCK, topics), 0) + rows.start
        column = lax.broadcasted_iota(jnp.int32, (BLOCK, topics), 1)
        return jnp.where(row == column, value, 0.0).astype(F32)

    def over_chunks(term):
        if chunks == 1:
            return term(0, slice(0, docs))

        def add(i, totals):
            terms = term(i, pl.ds(pl.multiple_of(i * chunk, chunk), chunk))
            return [total + one for total, one in zip(totals, terms)]

        return lax.fori_loop(0, chunks, add, [jnp.zeros((BLOCK, topics), F32) for _ in blocks])

    me = position()
    chain = docs // chains
    unit_rows = docs >> len(pairs)
    part_rows = unit_rows // chains

    def docs_of(i):
        place = lax.broadcasted_iota(jnp.int32, (1, chunk), 1) + i * chunk
        inside = lax.rem(place, chain)
        unit = unit_at(lax.div(inside, part_rows), me, pairs)
        return unit * unit_rows + lax.div(place, chain) * part_rows + lax.rem(inside, part_rows)

    def picked(i, docs_rows):
        hits = [(seeds_ref[rows, :] == docs_of(i)).astype(F32).astype(BF16) for rows in blocks]
        white = white_high[docs_rows, :]
        return [dot(hit, white, NN) for hit in hits]

    def moments(i, docs_rows):
        high, low = white_high[docs_rows, :], white_low[docs_rows, :]
        value = [dot(basis_high[rows, :], high, NT) + dot(basis_high[rows, :], low, NT) for rows in blocks]
        value = [split(v * v) for v in value]
        return [product(v, (high, low), NN) for v in value]

    def orthonormal(term, current):
        moment = over_chunks(term)
        norm = sum(jnp.sum(v * v) for v in moment)
        scale = topics * jnp.sqrt(norm / (topics * topics) + EPS)
        start = SHIFT / (SHIFT + 1.0)
        weight = 1.0 / ((SHIFT + 1.0) * scale)
        for v, rows in zip(moment, blocks):
            value = v * weight + start * current(rows)
            basis[rows, :] = value
            basis_high[rows, :], basis_low[rows, :] = split(value)
        both = (basis_high[...], basis_low[...])
        gram = [product((basis_high[rows, :], basis_low[rows, :]), both, NT) for rows in blocks]
        diff = [diagonal(rows, start * start) - g for g, rows in zip(gram, blocks)]
        e = 1.0 - start * start
        q = 1.0
        for pair in range(SWEEPS // 2):
            for step in range(2):
                for d, rows in zip(diff, blocks):
                    diff_high[rows, :] = d.astype(BF16)
                whole = diff_high[...]
                second = [dot(diff_high[rows, :], whole, NN) for rows in blocks]
                if pair < SWEEPS // 2 - 1:
                    third = [dot(v.astype(BF16), whole, NN) for v in second]
                if step == 0:
                    c0, c1, c2, c3, c4 = series(e)
                    value = [c1 * diff[k] + c2 * second[k] for k in each]
                    for v, rows in zip(second, blocks):
                        square_high[rows, :] = v.astype(BF16)
                    square = square_high[...]
                    mixed = [(c3 * diff[k] + c4 * second[k]).astype(BF16) for k in each]
                    value = [value[k] + dot(mixed[k], square, NN) for k in each]
                    if pair == 0:
                        factor = value
                        for f, rows in zip(factor, blocks):
                            factor_high[rows, :] = f.astype(BF16)
                    else:
                        before = factor_high[...]
                        factor = [
                            q * value[k] + c0 * factor[k] + dot(value[k].astype(BF16), before, NN) for k in each
                        ]
                    q = q * c0
                if pair == SWEEPS // 2 - 1:
                    break
                e, c1, c2, c3 = following(e)
                diff = [c1 * diff[k] + c2 * second[k] + c3 * third[k] for k in each]
        parts = [split(f) for f in factor]
        value = [q * basis[rows, :] + product(parts[k], both, NN) for k, rows in enumerate(blocks)]
        for v, rows in zip(value, blocks):
            basis[rows, :] = v
            basis_high[rows, :], basis_low[rows, :] = split(v)

    orthonormal(picked, lambda rows: diagonal(rows, 1.0))

    def turn(_, carry):
        orthonormal(moments, lambda rows: basis[rows, :])
        return carry

    lax.fori_loop(0, ITERS, turn, 0)
    parts = (basis_high[...], basis_low[...])
    total = jnp.zeros((1, topics), F32)
    for r in range(0, docs, chunk):
        value = product((white_high[r : r + chunk, :], white_low[r : r + chunk, :]), parts, NT)
        total += jnp.sum(value * value * value, axis=0, keepdims=True)
    weights_ref[...] = total / docs
    basis[...] = basis[...].T * math.sqrt(topics)
    own_rows = own_out.shape[0]
    own_out[...] = basis[pl.ds(pl.multiple_of(lax.axis_index("vocab") * own_rows, own_rows), own_rows), :]


def iterate(pieces, seeds, docs, pairs, own_rows):
    topics = seeds.shape[0]
    chunk = math.gcd(docs, 512)
    vmem = pl.BlockSpec(memory_space=pltpu.VMEM)
    return pl.pallas_call(
        functools.partial(iterate_kernel, chunk, pairs, CHAINS),
        in_specs=[vmem] * (1 + len(pieces)),
        out_specs=[vmem] * 2,
        out_shape=[
            jax.ShapeDtypeStruct((own_rows, topics), F32),
            jax.ShapeDtypeStruct((1, topics), F32),
        ],
        scratch_shapes=[
            pltpu.VMEM((topics, topics), F32),
            *[pltpu.VMEM((docs, topics), BF16)] * 2,
            *[pltpu.VMEM((topics, topics), BF16)] * 5,
        ],
        compiler_params=pltpu.CompilerParams(vmem_limit_bytes=40 << 20),
        name="iterate",
    )(seeds.reshape(topics, 1), *pieces)


CHAINS = 2
SCRATCH = 8
BLOCK = 256
VMEM_LIMIT = 53 << 20
CHUNKS = 4
AHEAD = 2
SWAP = True


def per_device(n_doc, n_vocab, count_tiles, tile_words, whitening, seeds):
    n = n_doc * n_vocab
    pairs, whole = plan(n_doc, n_vocab)
    halves = partial_rows(count_tiles[0], tile_words[0].T, whitening, pairs, CHAINS)
    rows, topics = halves[0].shape[0] * 2, whitening.shape[1]
    docs = rows * CHAINS
    values = [keep + exchange(send, pairs[0], n) for keep, send in zip(halves[::2], halves[1::2])]
    half = rows // 2
    for masks in pairs[1:]:
        half = half // 2
        values = [v[:half] + exchange(v[half:], masks, n) for v in values]
    for s in range(len(whole)):
        values = [v + exchange(v, whole[s ^ (c & 1) if SWAP else s], n) for c, v in enumerate(values)]
    for masks in reversed(pairs[1:]):
        values = [jnp.concatenate([v, exchange(v, masks, n)]) for v in values]
    pieces = []
    for v in values:
        pieces += [v, exchange(v, pairs[0], n)]
    directions, weights = iterate(pieces, seeds, docs, pairs, topics // n_vocab)
    return directions, weights.reshape(topics)


def solution(mesh):
    in_specs = (
        P(("doc", "vocab"), None, None, None, None),
        P(("doc", "vocab"), None, None),
        P(("doc", "vocab"), None),
        P(),
    )
    out_specs = (P("vocab", None), P())
    return jax.shard_map(
        functools.partial(per_device, mesh.shape["doc"], mesh.shape["vocab"]),
        mesh=mesh,
        in_specs=in_specs,
        out_specs=out_specs,
        check_vma=False,
    )
```

time: 66.4 us -> 63.5 us (0.956)
  Pallas kernels: 28.6 us -> 25.7 us
    pallas_call x1, Pallas kernels: 23.1 us -> 20.7 us  [iterate(): pl.pallas_call(functools.partial(iterate_kernel, chunk, pairs, CHAINS), i...]
where the time goes in v3:
time: 63.5 us; the launch traced here: 63.3 us
  Pallas kernels  25.7 us (40%)
  starting transfers between devices  23.7 us (37%)
  waiting for transfers between devices  12 us (19%)
  local copies, waits for them, and re-layouts  0.85 us (1%)
  between operations  0.78 us (1%)
    ppermute x16, starting transfers between devices, exchange(): return lax.ppermute(value, AXES, perm)  23.7 us
    pallas_call x1, Pallas kernels, iterate(): pl.pallas_call(functools.partial(iterate_kernel, chunk, pairs, CHAINS), i...  20.7 us
    ppermute x16, waiting for transfers between devices, exchange(): return lax.ppermute(value, AXES, perm)  12 us
    pallas_call x1, Pallas kernels, partial_rows(): pl.pallas_call(functools.partial(whiten_kernel, pairs, unit_blocks, half_...  5.01 us
  transfers between devices with their start and end apart: 16, of which 11 were waited for; matrix products, arithmetic and copies ran while one was open for 1% of the time, Pallas kernels for 0%

profile of v3, /device:TPU:0, one launch (start us, length us, event | category | flops | bytes accessed | tf_op | source)
XLA Modules:
  0.0 63.3 jit_solution(12369925477637619559)
XLA Ops:
  0.6 0.7 %copy-done = s32[1,32,2]{1,2,0:T(2,128)S(1)} copy-done((s32[1,32,2]{1,2,0:T(2,128)S(1)}, s32[1,32,2]{1,2,0:T(2,128)}, u32[]{:S(2)}) %copy-start) | copy-done | bytes 280
  1.3 5.0 %whiten.1 = (f32[128,512]{1,0:T(8,128)S(1)}, f32[128,512]{1,0:T(8,128)S(1)}, f32[128,512]{1,0:T(8,128)S(1)}, f32[128,512]{1,0:T(8,128)}) custom-call(s32[2,32]{1,0:T(2,128)S(1)} %bitcast.6, s32[32,2,16,128]{3,2,1,0:T(8,128)} %bitcast.7, bf16[4096,512]{1,0:T(8,128)(2,1)} %table.1), custom_call_target="tpu_custom_call" | custom-call | tf_op jit(solution)/shard_map/whiten/pallas_call | solution.py:131
  6.3 0.5 collective-permute-start.8
  6.8 0.1 collective-permute-start
  6.9 1.3 %collective-permute-done.8 = f32[128,512]{1,0:T(8,128)S(1)} collective-permute-done((f32[128,512]{1,0:T(8,128)}, f32[128,512]{1,0:T(8,128)S(1)}, u32[]{:S(2)}, u32[]{:S(2)}) %collective-permute-start.8) | collective-permute-done | bytes 262176 | tf_op jit(solution)/shard_map/ppermute | solution.py:64
  8.3 2.9 %collective-permute-start.9 = (f32[64,512]{1,0:T(8,128)S(1)}, f32[64,512]{1,0:T(8,128)S(1)}, u32[]{:S(2)}, u32[]{:S(2)}) collective-permute-start(f32[64,512]{1,0:T(8,128)S(1)} %slice.37), channel_id=1, source_target_pairs={{0,4},{1,3},{2,6},{3,1},{4,0},{5,7},{6,2},{7,5},{8,12},{9,11},{10,... | collective-permute-start | bytes 393224 | tf_op jit(solution)/shard_map/ppermute | solution.py:64
  11.3 0.1 collective-permute-start.1
  11.4 2.8 %collective-permute-done.9 = f32[64,512]{1,0:T(8,128)S(1)} collective-permute-done((f32[64,512]{1,0:T(8,128)S(1)}, f32[64,512]{1,0:T(8,128)S(1)}, u32[]{:S(2)}, u32[]{:S(2)}) %collective-permute-start.9) | collective-permute-done | bytes 131104 | tf_op jit(solution)/shard_map/ppermute | solution.py:64
  14.2 2.1 %collective-permute-start.10 = (f32[32,512]{1,0:T(8,128)S(1)}, f32[32,512]{1,0:T(8,128)S(1)}, u32[]{:S(2)}, u32[]{:S(2)}) collective-permute-start(f32[32,512]{1,0:T(8,128)S(1)} %slice.39), channel_id=1, source_target_pairs={{0,2},{1,5},{2,0},{3,7},{4,6},{5,1},{6,4},{7,3},{8,10},{9,13},{10,... | collective-permute-start | bytes 196616 | tf_op jit(solution)/shard_map/ppermute | solution.py:64
  16.3 0.0 collective-permute-done.1
  16.3 1.6 %collective-permute-start.2 = (f32[32,512]{1,0:T(8,128)S(1)}, f32[32,512]{1,0:T(8,128)S(1)}, u32[]{:S(2)}, u32[]{:S(2)}) collective-permute-start(f32[32,512]{1,0:T(8,128)S(1)} %slice.35), channel_id=1, source_target_pairs={{0,2},{1,5},{2,0},{3,7},{4,6},{5,1},{6,4},{7,3},{8,10},{9,13},{10,... | collective-permute-start | bytes 196616 | tf_op jit(solution)/shard_map/ppermute | solution.py:64
  17.9 0.6 collective-permute-done.10
  18.6 3.2 %collective-permute-start.11 = (f32[32,512]{1,0:T(8,128)S(1)}, f32[32,512]{1,0:T(8,128)S(1)}, u32[]{:S(2)}, u32[]{:S(2)}) collective-permute-start(f32[32,512]{1,0:T(8,128)S(1)} %slice_add_fusion.2), channel_id=1, source_target_pairs={{0,16},{1,17},{2,18},{3,19},{4,20},{5,21},{6,22},{7,23},{8,24},{9,... | collective-permute-start | bytes 196616 | tf_op jit(solution)/shard_map/ppermute | solution.py:64
  21.7 1.6 %collective-permute-start.3 = (f32[32,512]{1,0:T(8,128)S(1)}, f32[32,512]{1,0:T(8,128)S(1)}, u32[]{:S(2)}, u32[]{:S(2)}) collective-permute-start(f32[32,512]{1,0:T(8,128)S(1)} %slice_add_fusion.3), channel_id=1, source_target_pairs={{0,8},{1,9},{2,10},{3,11},{4,12},{5,13},{6,14},{7,15},{8,0},{9,1},... | collective-permute-start | bytes 196616 | tf_op jit(solution)/shard_map/ppermute | solution.py:64
  23.4 0.6 collective-permute-done.11
  24.0 2.0 %collective-permute-start.12 = (f32[32,512]{1,0:T(8,128)S(1)}, f32[32,512]{1,0:T(8,128)S(1)}, u32[]{:S(2)}, u32[]{:S(2)}) collective-permute-start(f32[32,512]{1,0:T(8,128)S(1)} %add.38), channel_id=1, source_target_pairs={{0,8},{1,9},{2,10},{3,11},{4,12},{5,13},{6,14},{7,15},{8,0},{9,1},... | collective-permute-start | bytes 196616 | tf_op jit(solution)/shard_map/ppermute | solution.py:64
  25.9 0.1 collective-permute-done.3
  26.1 3.2 %collective-permute-start.4 = (f32[32,512]{1,0:T(8,128)S(1)}, f32[32,512]{1,0:T(8,128)S(1)}, u32[]{:S(2)}, u32[]{:S(2)}) collective-permute-start(f32[32,512]{1,0:T(8,128)S(1)} %add.33), channel_id=1, source_target_pairs={{0,16},{1,17},{2,18},{3,19},{4,20},{5,21},{6,22},{7,23},{8,24},{9,... | collective-permute-start | bytes 196616 | tf_op jit(solution)/shard_map/ppermute | solution.py:64
  29.3 1.6 %collective-permute-start.13 = (f32[32,512]{1,0:T(8,128)S(1)}, f32[32,512]{1,0:T(8,128)S(1)}, u32[]{:S(2)}, u32[]{:S(2)}) collective-permute-start(f32[32,512]{1,0:T(8,128)S(1)} %add.39), channel_id=1, source_target_pairs={{0,2},{1,5},{2,0},{3,7},{4,6},{5,1},{6,4},{7,3},{8,10},{9,13},{10,... | collective-permute-start | bytes 196616 | tf_op jit(solution)/shard_map/ppermute | solution.py:64
  30.9 0.6 %collective-permute-done.4 = f32[32,512]{1,0:T(8,128)S(1)} collective-permute-done((f32[32,512]{1,0:T(8,128)S(1)}, f32[32,512]{1,0:T(8,128)S(1)}, u32[]{:S(2)}, u32[]{:S(2)}) %collective-permute-start.4) | collective-permute-done | bytes 65568 | tf_op jit(solution)/shard_map/ppermute | solution.py:64
  31.6 1.6 %collective-permute-start.5 = (f32[32,512]{1,0:T(8,128)S(1)}, f32[32,512]{1,0:T(8,128)S(1)}, u32[]{:S(2)}, u32[]{:S(2)}) collective-permute-start(f32[32,512]{1,0:T(8,128)S(1)} %add.34), channel_id=1, source_target_pairs={{0,2},{1,5},{2,0},{3,7},{4,6},{5,1},{6,4},{7,3},{8,10},{9,13},{10,... | collective-permute-start | bytes 196616 | tf_op jit(solution)/shard_map/ppermute | solution.py:64
  33.2 1.0 %collective-permute-done.13 = f32[32,512]{1,0:T(8,128)S(1)} collective-permute-done((f32[32,512]{1,0:T(8,128)S(1)}, f32[32,512]{1,0:T(8,128)S(1)}, u32[]{:S(2)}, u32[]{:S(2)}) %collective-permute-start.13) | collective-permute-done | bytes 65568 | tf_op jit(solution)/shard_map/ppermute | solution.py:64
  34.1 1.5 %collective-permute-start.14 = (f32[64,512]{1,0:T(8,128)S(1)}, f32[64,512]{1,0:T(8,128)S(1)}, u32[]{:S(2)}, u32[]{:S(2)}) collective-permute-start(f32[64,512]{1,0:T(8,128)S(1)} %pad_maximum_fusion.3), channel_id=1, source_target_pairs={{0,4},{1,3},{2,6},{3,1},{4,0},{5,7},{6,2},{7,5},{8,12},{9,11},{10,... | collective-permute-start | bytes 393224 | tf_op jit(solution)/shard_map/ppermute | solution.py:64
  35.7 0.2 collective-permute-done.5
  35.9 1.6 %collective-permute-start.6 = (f32[64,512]{1,0:T(8,128)S(1)}, f32[64,512]{1,0:T(8,128)S(1)}, u32[]{:S(2)}, u32[]{:S(2)}) collective-permute-start(f32[64,512]{1,0:T(8,128)S(1)} %pad_maximum_fusion.2), channel_id=1, source_target_pairs={{0,4},{1,3},{2,6},{3,1},{4,0},{5,7},{6,2},{7,5},{8,12},{9,11},{10,... | collective-permute-start | bytes 393224 | tf_op jit(solution)/shard_map/ppermute | solution.py:64
  37.5 1.7 %collective-permute-done.14 = f32[64,512]{1,0:T(8,128)S(1)} collective-permute-done((f32[64,512]{1,0:T(8,128)S(1)}, f32[64,512]{1,0:T(8,128)S(1)}, u32[]{:S(2)}, u32[]{:S(2)}) %collective-permute-start.14) | collective-permute-done | bytes 131104 | tf_op jit(solution)/shard_map/ppermute | solution.py:64
  39.2 0.1 collective-permute-start.15
  39.3 1.7 %collective-permute-done.6 = f32[64,512]{1,0:T(8,128)S(1)} collective-permute-done((f32[64,512]{1,0:T(8,128)S(1)}, f32[64,512]{1,0:T(8,128)S(1)}, u32[]{:S(2)}, u32[]{:S(2)}) %collective-permute-start.6) | collective-permute-done | bytes 131104 | tf_op jit(solution)/shard_map/ppermute | solution.py:64
  41.0 0.1 collective-permute-start.7
  41.1 0.1 copy.6.seeds_ref
  41.2 1.3 %collective-permute-done.7.rest_1_ = f32[128,512]{1,0:T(8,128)S(1)} collective-permute-done((f32[128,512]{1,0:T(8,128)S(1)}, f32[128,512]{1,0:T(8,128)S(1)}, u32[]{:S(2)}, u32[]{:S(2)}) %collective-permute-start.7) | collective-permute-done | bytes 262176 | tf_op jit(solution)/shard_map/ppermute | solution.py:64
  42.6 20.7 %iterate.1 = (f32[128,512]{1,0:T(8,128)}, f32[1,512]{1,0:T(1,128)}) custom-call(s32[512,1]{1,0:T(8,128)S(1)} %copy.6.seeds_ref, f32[128,512]{1,0:T(8,128)S(1)} %pad_maximum_fusion.rest_0_, f32[128,512]{1,0:T(8,128)S(1)} %collective-permute-done.7.rest_1_, f32[128,512]{1,0:T(8,128)S(1)} %pad_maximum_fusion.1.rest_2_, ...), custom_call_target="tpu_custom_call" | custom-call | tf_op jit(solution)/shard_map/iterate/pallas_call | solution.py:293
  (25 shorter events, 0.3 us)
Async XLA Ops:
  0.6 0.7 %copy-start = (s32[1,32,2]{1,2,0:T(2,128)S(1)}, s32[1,32,2]{1,2,0:T(2,128)}, u32[]{:S(2)}) copy-start(s32[1,32,2]{1,2,0:T(2,128)} %param.5) | copy-start | bytes 772
  1.3 39.7 %copy-start.1 = (s32[512]{0:T(512)S(1)}, s32[512]{0:T(512)}, u32[]{:S(2)}) copy-start(s32[512]{0:T(512)} %param.7) | copy-start | bytes 6148
  6.3 1.9 %collective-permute-start.8 = (f32[128,512]{1,0:T(8,128)}, f32[128,512]{1,0:T(8,128)S(1)}, u32[]{:S(2)}, u32[]{:S(2)}) collective-permute-start(f32[128,512]{1,0:T(8,128)} %get-tuple-element.11), channel_id=1, source_target_pairs={{0,1},{1,0},{2,3},{3,2},{4,5},{5,4},{6,7},{7,6},{8,9},{9,8},{10,11... | collective-permute-start | bytes 786440 | tf_op jit(solution)/shard_map/ppermute | solution.py:64
  6.8 4.4 %collective-permute-start = (f32[128,512]{1,0:T(8,128)S(1)}, f32[128,512]{1,0:T(8,128)S(1)}, u32[]{:S(2)}, u32[]{:S(2)}) collective-permute-start(f32[128,512]{1,0:T(8,128)S(1)} %get-tuple-element.9), channel_id=1, source_target_pairs={{0,1},{1,0},{2,3},{3,2},{4,5},{5,4},{6,7},{7,6},{8,9},{9,8},{10,11... | collective-permute-start | bytes 786440 | tf_op jit(solution)/shard_map/ppermute | solution.py:64
  8.3 5.9 %collective-permute-start.9 = (f32[64,512]{1,0:T(8,128)S(1)}, f32[64,512]{1,0:T(8,128)S(1)}, u32[]{:S(2)}, u32[]{:S(2)}) collective-permute-start(f32[64,512]{1,0:T(8,128)S(1)} %slice.37), channel_id=1, source_target_pairs={{0,4},{1,3},{2,6},{3,1},{4,0},{5,7},{6,2},{7,5},{8,12},{9,11},{10,... | collective-permute-start | bytes 393224 | tf_op jit(solution)/shard_map/ppermute | solution.py:64
  11.3 5.0 %collective-permute-start.1 = (f32[64,512]{1,0:T(8,128)S(1)}, f32[64,512]{1,0:T(8,128)S(1)}, u32[]{:S(2)}, u32[]{:S(2)}) collective-permute-start(f32[64,512]{1,0:T(8,128)S(1)} %slice.33), channel_id=1, source_target_pairs={{0,4},{1,3},{2,6},{3,1},{4,0},{5,7},{6,2},{7,5},{8,12},{9,11},{10,... | collective-permute-start | bytes 393224 | tf_op jit(solution)/shard_map/ppermute | solution.py:64
  14.2 4.4 %collective-permute-start.10 = (f32[32,512]{1,0:T(8,128)S(1)}, f32[32,512]{1,0:T(8,128)S(1)}, u32[]{:S(2)}, u32[]{:S(2)}) collective-permute-start(f32[32,512]{1,0:T(8,128)S(1)} %slice.39), channel_id=1, source_target_pairs={{0,2},{1,5},{2,0},{3,7},{4,6},{5,1},{6,4},{7,3},{8,10},{9,13},{10,... | collective-permute-start | bytes 196616 | tf_op jit(solution)/shard_map/ppermute | solution.py:64
  16.3 5.4 %collective-permute-start.2 = (f32[32,512]{1,0:T(8,128)S(1)}, f32[32,512]{1,0:T(8,128)S(1)}, u32[]{:S(2)}, u32[]{:S(2)}) collective-permute-start(f32[32,512]{1,0:T(8,128)S(1)} %slice.35), channel_id=1, source_target_pairs={{0,2},{1,5},{2,0},{3,7},{4,6},{5,1},{6,4},{7,3},{8,10},{9,13},{10,... | collective-permute-start | bytes 196616 | tf_op jit(solution)/shard_map/ppermute | solution.py:64
  18.6 5.4 %collective-permute-start.11 = (f32[32,512]{1,0:T(8,128)S(1)}, f32[32,512]{1,0:T(8,128)S(1)}, u32[]{:S(2)}, u32[]{:S(2)}) collective-permute-start(f32[32,512]{1,0:T(8,128)S(1)} %slice_add_fusion.2), channel_id=1, source_target_pairs={{0,16},{1,17},{2,18},{3,19},{4,20},{5,21},{6,22},{7,23},{8,24},{9,... | collective-permute-start | bytes 196616 | tf_op jit(solution)/shard_map/ppermute | solution.py:64
  21.7 4.3 %collective-permute-start.3 = (f32[32,512]{1,0:T(8,128)S(1)}, f32[32,512]{1,0:T(8,128)S(1)}, u32[]{:S(2)}, u32[]{:S(2)}) collective-permute-start(f32[32,512]{1,0:T(8,128)S(1)} %slice_add_fusion.3), channel_id=1, source_target_pairs={{0,8},{1,9},{2,10},{3,11},{4,12},{5,13},{6,14},{7,15},{8,0},{9,1},... | collective-permute-start | bytes 196616 | tf_op jit(solution)/shard_map/ppermute | solution.py:64
  24.0 5.3 %collective-permute-start.12 = (f32[32,512]{1,0:T(8,128)S(1)}, f32[32,512]{1,0:T(8,128)S(1)}, u32[]{:S(2)}, u32[]{:S(2)}) collective-permute-start(f32[32,512]{1,0:T(8,128)S(1)} %add.38), channel_id=1, source_target_pairs={{0,8},{1,9},{2,10},{3,11},{4,12},{5,13},{6,14},{7,15},{8,0},{9,1},... | collective-permute-start | bytes 196616 | tf_op jit(solution)/shard_map/ppermute | solution.py:64
  26.1 5.5 %collective-permute-start.4 = (f32[32,512]{1,0:T(8,128)S(1)}, f32[32,512]{1,0:T(8,128)S(1)}, u32[]{:S(2)}, u32[]{:S(2)}) collective-permute-start(f32[32,512]{1,0:T(8,128)S(1)} %add.33), channel_id=1, source_target_pairs={{0,16},{1,17},{2,18},{3,19},{4,20},{5,21},{6,22},{7,23},{8,24},{9,... | collective-permute-start | bytes 196616 | tf_op jit(solution)/shard_map/ppermute | solution.py:64
  29.3 4.8 %collective-permute-start.13 = (f32[32,512]{1,0:T(8,128)S(1)}, f32[32,512]{1,0:T(8,128)S(1)}, u32[]{:S(2)}, u32[]{:S(2)}) collective-permute-start(f32[32,512]{1,0:T(8,128)S(1)} %add.39), channel_id=1, source_target_pairs={{0,2},{1,5},{2,0},{3,7},{4,6},{5,1},{6,4},{7,3},{8,10},{9,13},{10,... | collective-permute-start | bytes 196616 | tf_op jit(solution)/shard_map/ppermute | solution.py:64
  31.6 4.3 %collective-permute-start.5 = (f32[32,512]{1,0:T(8,128)S(1)}, f32[32,512]{1,0:T(8,128)S(1)}, u32[]{:S(2)}, u32[]{:S(2)}) collective-permute-start(f32[32,512]{1,0:T(8,128)S(1)} %add.34), channel_id=1, source_target_pairs={{0,2},{1,5},{2,0},{3,7},{4,6},{5,1},{6,4},{7,3},{8,10},{9,13},{10,... | collective-permute-start | bytes 196616 | tf_op jit(solution)/shard_map/ppermute | solution.py:64
  34.1 5.0 %collective-permute-start.14 = (f32[64,512]{1,0:T(8,128)S(1)}, f32[64,512]{1,0:T(8,128)S(1)}, u32[]{:S(2)}, u32[]{:S(2)}) collective-permute-start(f32[64,512]{1,0:T(8,128)S(1)} %pad_maximum_fusion.3), channel_id=1, source_target_pairs={{0,4},{1,3},{2,6},{3,1},{4,0},{5,7},{6,2},{7,5},{8,12},{9,11},{10,... | collective-permute-start | bytes 393224 | tf_op jit(solution)/shard_map/ppermute | solution.py:64
  35.9 5.0 %collective-permute-start.6 = (f32[64,512]{1,0:T(8,128)S(1)}, f32[64,512]{1,0:T(8,128)S(1)}, u32[]{:S(2)}, u32[]{:S(2)}) collective-permute-start(f32[64,512]{1,0:T(8,128)S(1)} %pad_maximum_fusion.2), channel_id=1, source_target_pairs={{0,4},{1,3},{2,6},{3,1},{4,0},{5,7},{6,2},{7,5},{8,12},{9,11},{10,... | collective-permute-start | bytes 393224 | tf_op jit(solution)/shard_map/ppermute | solution.py:64
  39.2 2.0 %collective-permute-start.15 = (f32[128,512]{1,0:T(8,128)S(1)}, f32[128,512]{1,0:T(8,128)S(1)}, u32[]{:S(2)}, u32[]{:S(2)}) collective-permute-start(f32[128,512]{1,0:T(8,128)S(1)} %pad_maximum_fusion.1.rest_2_), channel_id=1, source_target_pairs={{0,1},{1,0},{2,3},{3,2},{4,5},{5,4},{6,7},{7,6},{8,9},{9,8},{10,11... | collective-permute-start | bytes 786440 | tf_op jit(solution)/shard_map/ppermute | solution.py:64
  41.0 1.6 %collective-permute-start.7 = (f32[128,512]{1,0:T(8,128)S(1)}, f32[128,512]{1,0:T(8,128)S(1)}, u32[]{:S(2)}, u32[]{:S(2)}) collective-permute-start(f32[128,512]{1,0:T(8,128)S(1)} %pad_maximum_fusion.rest_0_), channel_id=1, source_target_pairs={{0,1},{1,0},{2,3},{3,2},{4,5},{5,4},{6,7},{7,6},{8,9},{9,8},{10,11... | collective-permute-start | bytes 786440 | tf_op jit(solution)/shard_map/ppermute | solution.py:64

commit v4 on v3

--- a/solution.py
+++ b/solution.py
@@ -219,7 +219,8 @@
 
     def orthonormal(term, current):
         moment = over_chunks(term)
-        norm = sum(jnp.sum(v * v) for v in moment)
+        norm = sum(jnp.sum(v * v, axis=0, keepdims=True) for v in moment)
+        norm = jnp.sum(norm, axis=1, keepdims=True)
         scale = topics * jnp.sqrt(norm / (topics * topics) + EPS)
         start = SHIFT / (SHIFT + 1.0)
         weight = 1.0 / ((SHIFT + 1.0) * scale)
@@ -228,7 +229,9 @@
             basis[rows, :] = value
             basis_high[rows, :], basis_low[rows, :] = split(value)
         both = (basis_high[...], basis_low[...])
-        gram = [product((basis_high[rows, :], basis_low[rows, :]), both, NT) for rows in blocks]
+        cross = dot(both[0], both[1], NT)
+        gram = dot(both[0], both[0], NT) + (cross + cross.T)
+        gram = [gram[rows, :] for rows in blocks]
         diff = [diagonal(rows, start * start) - g for g, rows in zip(gram, blocks)]
         e = 1.0 - start * start
         q = 1.0
@@ -270,11 +273,8 @@
 
     orthonormal(picked, lambda rows: diagonal(rows, 1.0))
 
-    def turn(_, carry):
+    for _ in range(ITERS):
         orthonormal(moments, lambda rows: basis[rows, :])
-        return carry
-
-    lax.fori_loop(0, ITERS, turn, 0)
     parts = (basis_high[...], basis_low[...])
     total = jnp.zeros((1, topics), F32)
     for r in range(0, docs, chunk):
@@ -330,11 +330,12 @@
         values = [v[:half] + exchange(v[half:], masks, n) for v in values]
     for s in range(len(whole)):
         values = [v + exchange(v, whole[s ^ (c & 1) if SWAP else s], n) for c, v in enumerate(values)]
-    for masks in reversed(pairs[1:]):
+    for masks in reversed(pairs[2:]):
         values = [jnp.concatenate([v, exchange(v, masks, n)]) for v in values]
     pieces = []
     for v in values:
-        pieces += [v, exchange(v, pairs[0], n)]
+        rest = exchange(v, pairs[1], n)
+        pieces += [v, rest, exchange(v, pairs[0], n), exchange(rest, pairs[0], n)]
     directions, weights = iterate(pieces, seeds, docs, pairs, topics // n_vocab)
     return directions, weights.reshape(topics)
 

time: 63.5 us -> 61 us (0.961)
  Pallas kernels: 25.7 us -> 23.6 us
    pallas_call x1, Pallas kernels: 20.7 us -> 18.5 us  [iterate(): pl.pallas_call(functools.partial(iterate_kernel, chunk, pairs, CHAINS), i...]
    ppermute x16 -> x18, waiting for transfers between devices: 12 us -> 11.4 us  [exchange(): return lax.ppermute(value, AXES, perm)]
    ppermute x16 -> x18, starting transfers between devices: 23.7 us -> 24.1 us  [exchange(): return lax.ppermute(value, AXES, perm)]
  transfers between devices with their start and end apart: 16 -> 18, of which waited for: 11 -> 11; matrix products, arithmetic and copies ran while one was open for 1% -> 1% of each run, Pallas kernels for 0% -> 0%
where the time goes in v4:
time: 61 us; the launch traced here: 60.8 us
  starting transfers between devices  24.1 us (40%)
  Pallas kernels  23.6 us (39%)
  waiting for transfers between devices  11.4 us (19%)
  local copies, waits for them, and re-layouts  0.85 us (1%)
  between operations  0.77 us (1%)
    ppermute x18, starting transfers between devices, exchange(): return lax.ppermute(value, AXES, perm)  24.1 us
    pallas_call x1, Pallas kernels, iterate(): pl.pallas_call(functools.partial(iterate_kernel, chunk, pairs, CHAINS), i...  18.5 us
    ppermute x18, waiting for transfers between devices, exchange(): return lax.ppermute(value, AXES, perm)  11.4 us
    pallas_call x1, Pallas kernels, partial_rows(): pl.pallas_call(functools.partial(whiten_kernel, pairs, unit_blocks, half_...  5.01 us
  transfers between devices with their start and end apart: 18, of which 11 were waited for; matrix products, arithmetic and copies ran while one was open for 1% of the time, Pallas kernels for 0%

profile of v4, /device:TPU:0, one launch (start us, length us, event | category | flops | bytes accessed | tf_op | source)
XLA Modules:
  0.0 60.8 jit_solution(17218288965781046624)
XLA Ops:
  0.6 0.7 %copy-done = s32[1,32,2]{1,2,0:T(2,128)S(1)} copy-done((s32[1,32,2]{1,2,0:T(2,128)S(1)}, s32[1,32,2]{1,2,0:T(2,128)}, u32[]{:S(2)}) %copy-start) | copy-done | bytes 280
  1.3 5.0 %whiten.1 = (f32[128,512]{1,0:T(8,128)S(1)}, f32[128,512]{1,0:T(8,128)S(1)}, f32[128,512]{1,0:T(8,128)S(1)}, f32[128,512]{1,0:T(8,128)}) custom-call(s32[2,32]{1,0:T(2,128)S(1)} %bitcast.6, s32[32,2,16,128]{3,2,1,0:T(8,128)} %bitcast.7, bf16[4096,512]{1,0:T(8,128)(2,1)} %table.1), custom_call_target="tpu_custom_call" | custom-call | tf_op jit(solution)/shard_map/whiten/pallas_call | solution.py:131
  6.3 0.5 collective-permute-start.9
  6.8 0.1 collective-permute-start
  6.9 1.3 %collective-permute-done.9 = f32[128,512]{1,0:T(8,128)S(1)} collective-permute-done((f32[128,512]{1,0:T(8,128)}, f32[128,512]{1,0:T(8,128)S(1)}, u32[]{:S(2)}, u32[]{:S(2)}) %collective-permute-start.9) | collective-permute-done | bytes 262176 | tf_op jit(solution)/shard_map/ppermute | solution.py:64
  8.3 2.9 %collective-permute-start.10 = (f32[64,512]{1,0:T(8,128)S(1)}, f32[64,512]{1,0:T(8,128)S(1)}, u32[]{:S(2)}, u32[]{:S(2)}) collective-permute-start(f32[64,512]{1,0:T(8,128)S(1)} %slice.37), channel_id=1, source_target_pairs={{0,4},{1,3},{2,6},{3,1},{4,0},{5,7},{6,2},{7,5},{8,12},{9,11},{10,... | collective-permute-start | bytes 393224 | tf_op jit(solution)/shard_map/ppermute | solution.py:64
  11.2 0.0 collective-permute-done
  11.3 0.1 collective-permute-start.1
  11.4 2.8 %collective-permute-done.10 = f32[64,512]{1,0:T(8,128)S(1)} collective-permute-done((f32[64,512]{1,0:T(8,128)S(1)}, f32[64,512]{1,0:T(8,128)S(1)}, u32[]{:S(2)}, u32[]{:S(2)}) %collective-permute-start.10) | collective-permute-done | bytes 131104 | tf_op jit(solution)/shard_map/ppermute | solution.py:64
  14.2 2.1 %collective-permute-start.11 = (f32[32,512]{1,0:T(8,128)S(1)}, f32[32,512]{1,0:T(8,128)S(1)}, u32[]{:S(2)}, u32[]{:S(2)}) collective-permute-start(f32[32,512]{1,0:T(8,128)S(1)} %slice.39), channel_id=1, source_target_pairs={{0,2},{1,5},{2,0},{3,7},{4,6},{5,1},{6,4},{7,3},{8,10},{9,13},{10,... | collective-permute-start | bytes 196616 | tf_op jit(solution)/shard_map/ppermute | solution.py:64
  16.3 1.6 %collective-permute-start.2 = (f32[32,512]{1,0:T(8,128)S(1)}, f32[32,512]{1,0:T(8,128)S(1)}, u32[]{:S(2)}, u32[]{:S(2)}) collective-permute-start(f32[32,512]{1,0:T(8,128)S(1)} %slice.35), channel_id=1, source_target_pairs={{0,2},{1,5},{2,0},{3,7},{4,6},{5,1},{6,4},{7,3},{8,10},{9,13},{10,... | collective-permute-start | bytes 196616 | tf_op jit(solution)/shard_map/ppermute | solution.py:64
  17.9 0.6 %collective-permute-done.11 = f32[32,512]{1,0:T(8,128)S(1)} collective-permute-done((f32[32,512]{1,0:T(8,128)S(1)}, f32[32,512]{1,0:T(8,128)S(1)}, u32[]{:S(2)}, u32[]{:S(2)}) %collective-permute-start.11) | collective-permute-done | bytes 65568 | tf_op jit(solution)/shard_map/ppermute | solution.py:64
  18.6 3.2 %collective-permute-start.12 = (f32[32,512]{1,0:T(8,128)S(1)}, f32[32,512]{1,0:T(8,128)S(1)}, u32[]{:S(2)}, u32[]{:S(2)}) collective-permute-start(f32[32,512]{1,0:T(8,128)S(1)} %slice_add_fusion.2), channel_id=1, source_target_pairs={{0,16},{1,17},{2,18},{3,19},{4,20},{5,21},{6,22},{7,23},{8,24},{9,... | collective-permute-start | bytes 196616 | tf_op jit(solution)/shard_map/ppermute | solution.py:64
  21.7 0.0 collective-permute-done.2
  21.7 1.6 %collective-permute-start.3 = (f32[32,512]{1,0:T(8,128)S(1)}, f32[32,512]{1,0:T(8,128)S(1)}, u32[]{:S(2)}, u32[]{:S(2)}) collective-permute-start(f32[32,512]{1,0:T(8,128)S(1)} %slice_add_fusion.3), channel_id=1, source_target_pairs={{0,8},{1,9},{2,10},{3,11},{4,12},{5,13},{6,14},{7,15},{8,0},{9,1},... | collective-permute-start | bytes 196616 | tf_op jit(solution)/shard_map/ppermute | solution.py:64
  23.4 0.6 collective-permute-done.12
  24.0 2.0 %collective-permute-start.13 = (f32[32,512]{1,0:T(8,128)S(1)}, f32[32,512]{1,0:T(8,128)S(1)}, u32[]{:S(2)}, u32[]{:S(2)}) collective-permute-start(f32[32,512]{1,0:T(8,128)S(1)} %add.38), channel_id=1, source_target_pairs={{0,8},{1,9},{2,10},{3,11},{4,12},{5,13},{6,14},{7,15},{8,0},{9,1},... | collective-permute-start | bytes 196616 | tf_op jit(solution)/shard_map/ppermute | solution.py:64
  25.9 0.1 collective-permute-done.3
  26.1 3.2 %collective-permute-start.4 = (f32[32,512]{1,0:T(8,128)S(1)}, f32[32,512]{1,0:T(8,128)S(1)}, u32[]{:S(2)}, u32[]{:S(2)}) collective-permute-start(f32[32,512]{1,0:T(8,128)S(1)} %add.33), channel_id=1, source_target_pairs={{0,16},{1,17},{2,18},{3,19},{4,20},{5,21},{6,22},{7,23},{8,24},{9,... | collective-permute-start | bytes 196616 | tf_op jit(solution)/shard_map/ppermute | solution.py:64
  29.3 1.6 %collective-permute-start.14 = (f32[32,512]{1,0:T(8,128)S(1)}, f32[32,512]{1,0:T(8,128)S(1)}, u32[]{:S(2)}, u32[]{:S(2)}) collective-permute-start(f32[32,512]{1,0:T(8,128)S(1)} %add.39), channel_id=1, source_target_pairs={{0,2},{1,5},{2,0},{3,7},{4,6},{5,1},{6,4},{7,3},{8,10},{9,13},{10,... | collective-permute-start | bytes 196616 | tf_op jit(solution)/shard_map/ppermute | solution.py:64
  30.9 0.6 %collective-permute-done.4 = f32[32,512]{1,0:T(8,128)S(1)} collective-permute-done((f32[32,512]{1,0:T(8,128)S(1)}, f32[32,512]{1,0:T(8,128)S(1)}, u32[]{:S(2)}, u32[]{:S(2)}) %collective-permute-start.4) | collective-permute-done | bytes 65568 | tf_op jit(solution)/shard_map/ppermute | solution.py:64
  31.6 1.6 %collective-permute-start.5 = (f32[32,512]{1,0:T(8,128)S(1)}, f32[32,512]{1,0:T(8,128)S(1)}, u32[]{:S(2)}, u32[]{:S(2)}) collective-permute-start(f32[32,512]{1,0:T(8,128)S(1)} %add.34), channel_id=1, source_target_pairs={{0,2},{1,5},{2,0},{3,7},{4,6},{5,1},{6,4},{7,3},{8,10},{9,13},{10,... | collective-permute-start | bytes 196616 | tf_op jit(solution)/shard_map/ppermute | solution.py:64
  33.2 1.0 %collective-permute-done.14 = f32[32,512]{1,0:T(8,128)S(1)} collective-permute-done((f32[32,512]{1,0:T(8,128)S(1)}, f32[32,512]{1,0:T(8,128)S(1)}, u32[]{:S(2)}, u32[]{:S(2)}) %collective-permute-start.14) | collective-permute-done | bytes 65568 | tf_op jit(solution)/shard_map/ppermute | solution.py:64
  34.1 1.6 %collective-permute-start.15 = (f32[64,512]{1,0:T(8,128)S(1)}, f32[64,512]{1,0:T(8,128)S(1)}, u32[]{:S(2)}, u32[]{:S(2)}) collective-permute-start(f32[64,512]{1,0:T(8,128)S(1)} %pad_maximum_fusion.1.rest_4_), channel_id=1, source_target_pairs={{0,4},{1,3},{2,6},{3,1},{4,0},{5,7},{6,2},{7,5},{8,12},{9,11},{10,... | collective-permute-start | bytes 393224 | tf_op jit(solution)/shard_map/ppermute | solution.py:64
  35.7 0.2 collective-permute-done.5
  35.9 1.6 %collective-permute-start.6 = (f32[64,512]{1,0:T(8,128)S(1)}, f32[64,512]{1,0:T(8,128)S(1)}, u32[]{:S(2)}, u32[]{:S(2)}) collective-permute-start(f32[64,512]{1,0:T(8,128)S(1)} %pad_maximum_fusion.rest_0_), channel_id=1, source_target_pairs={{0,4},{1,3},{2,6},{3,1},{4,0},{5,7},{6,2},{7,5},{8,12},{9,11},{10,... | collective-permute-start | bytes 393224 | tf_op jit(solution)/shard_map/ppermute | solution.py:64
  37.5 0.5 collective-permute-start.7
  38.0 1.2 %collective-permute-done.15.rest_5_ = f32[64,512]{1,0:T(8,128)S(1)} collective-permute-done((f32[64,512]{1,0:T(8,128)S(1)}, f32[64,512]{1,0:T(8,128)S(1)}, u32[]{:S(2)}, u32[]{:S(2)}) %collective-permute-start.15) | collective-permute-done | bytes 131104 | tf_op jit(solution)/shard_map/ppermute | solution.py:64
  39.2 1.8 %collective-permute-done.6.rest_1_ = f32[64,512]{1,0:T(8,128)S(1)} collective-permute-done((f32[64,512]{1,0:T(8,128)S(1)}, f32[64,512]{1,0:T(8,128)S(1)}, u32[]{:S(2)}, u32[]{:S(2)}) %collective-permute-start.6) | collective-permute-done | bytes 131104 | tf_op jit(solution)/shard_map/ppermute | solution.py:64
  41.0 0.1 copy.6.seeds_ref
  41.1 1.2 %collective-permute-done.8.rest_3_ = f32[64,512]{1,0:T(8,128)S(1)} collective-permute-done((f32[64,512]{1,0:T(8,128)S(1)}, f32[64,512]{1,0:T(8,128)S(1)}, u32[]{:S(2)}, u32[]{:S(2)}) %collective-permute-start.8) | collective-permute-done | bytes 131104 | tf_op jit(solution)/shard_map/ppermute | solution.py:64
  42.3 18.5 %iterate.1 = (f32[128,512]{1,0:T(8,128)}, f32[1,512]{1,0:T(1,128)}) custom-call(s32[512,1]{1,0:T(8,128)S(1)} %copy.6.seeds_ref, f32[64,512]{1,0:T(8,128)S(1)} %pad_maximum_fusion.rest_0_, f32[64,512]{1,0:T(8,128)S(1)} %collective-permute-done.6.rest_1_, f32[64,512]{1,0:T(8,128)S(1)} %collective-permute-done.7.rest_2_, ...), custom_call_target="tpu_custom_call" | custom-call | tf_op jit(solution)/shard_map/iterate/pallas_call | solution.py:293
  (27 shorter events, 0.3 us)
Async XLA Ops:
  0.6 0.7 %copy-start = (s32[1,32,2]{1,2,0:T(2,128)S(1)}, s32[1,32,2]{1,2,0:T(2,128)}, u32[]{:S(2)}) copy-start(s32[1,32,2]{1,2,0:T(2,128)} %param.5) | copy-start | bytes 772
  1.3 39.6 %copy-start.1 = (s32[512]{0:T(512)S(1)}, s32[512]{0:T(512)}, u32[]{:S(2)}) copy-start(s32[512]{0:T(512)} %param.7) | copy-start | bytes 6148
  6.3 1.9 %collective-permute-start.9 = (f32[128,512]{1,0:T(8,128)}, f32[128,512]{1,0:T(8,128)S(1)}, u32[]{:S(2)}, u32[]{:S(2)}) collective-permute-start(f32[128,512]{1,0:T(8,128)} %get-tuple-element.11), channel_id=1, source_target_pairs={{0,1},{1,0},{2,3},{3,2},{4,5},{5,4},{6,7},{7,6},{8,9},{9,8},{10,11... | collective-permute-start | bytes 786440 | tf_op jit(solution)/shard_map/ppermute | solution.py:64
  6.8 4.4 %collective-permute-start = (f32[128,512]{1,0:T(8,128)S(1)}, f32[128,512]{1,0:T(8,128)S(1)}, u32[]{:S(2)}, u32[]{:S(2)}) collective-permute-start(f32[128,512]{1,0:T(8,128)S(1)} %get-tuple-element.9), channel_id=1, source_target_pairs={{0,1},{1,0},{2,3},{3,2},{4,5},{5,4},{6,7},{7,6},{8,9},{9,8},{10,11... | collective-permute-start | bytes 786440 | tf_op jit(solution)/shard_map/ppermute | solution.py:64
  8.3 5.9 %collective-permute-start.10 = (f32[64,512]{1,0:T(8,128)S(1)}, f32[64,512]{1,0:T(8,128)S(1)}, u32[]{:S(2)}, u32[]{:S(2)}) collective-permute-start(f32[64,512]{1,0:T(8,128)S(1)} %slice.37), channel_id=1, source_target_pairs={{0,4},{1,3},{2,6},{3,1},{4,0},{5,7},{6,2},{7,5},{8,12},{9,11},{10,... | collective-permute-start | bytes 393224 | tf_op jit(solution)/shard_map/ppermute | solution.py:64
  11.3 5.0 %collective-permute-start.1 = (f32[64,512]{1,0:T(8,128)S(1)}, f32[64,512]{1,0:T(8,128)S(1)}, u32[]{:S(2)}, u32[]{:S(2)}) collective-permute-start(f32[64,512]{1,0:T(8,128)S(1)} %slice.33), channel_id=1, source_target_pairs={{0,4},{1,3},{2,6},{3,1},{4,0},{5,7},{6,2},{7,5},{8,12},{9,11},{10,... | collective-permute-start | bytes 393224 | tf_op jit(solution)/shard_map/ppermute | solution.py:64
  14.2 4.4 %collective-permute-start.11 = (f32[32,512]{1,0:T(8,128)S(1)}, f32[32,512]{1,0:T(8,128)S(1)}, u32[]{:S(2)}, u32[]{:S(2)}) collective-permute-start(f32[32,512]{1,0:T(8,128)S(1)} %slice.39), channel_id=1, source_target_pairs={{0,2},{1,5},{2,0},{3,7},{4,6},{5,1},{6,4},{7,3},{8,10},{9,13},{10,... | collective-permute-start | bytes 196616 | tf_op jit(solution)/shard_map/ppermute | solution.py:64
  16.3 5.4 %collective-permute-start.2 = (f32[32,512]{1,0:T(8,128)S(1)}, f32[32,512]{1,0:T(8,128)S(1)}, u32[]{:S(2)}, u32[]{:S(2)}) collective-permute-start(f32[32,512]{1,0:T(8,128)S(1)} %slice.35), channel_id=1, source_target_pairs={{0,2},{1,5},{2,0},{3,7},{4,6},{5,1},{6,4},{7,3},{8,10},{9,13},{10,... | collective-permute-start | bytes 196616 | tf_op jit(solution)/shard_map/ppermute | solution.py:64
  18.6 5.4 %collective-permute-start.12 = (f32[32,512]{1,0:T(8,128)S(1)}, f32[32,512]{1,0:T(8,128)S(1)}, u32[]{:S(2)}, u32[]{:S(2)}) collective-permute-start(f32[32,512]{1,0:T(8,128)S(1)} %slice_add_fusion.2), channel_id=1, source_target_pairs={{0,16},{1,17},{2,18},{3,19},{4,20},{5,21},{6,22},{7,23},{8,24},{9,... | collective-permute-start | bytes 196616 | tf_op jit(solution)/shard_map/ppermute | solution.py:64
  21.7 4.3 %collective-permute-start.3 = (f32[32,512]{1,0:T(8,128)S(1)}, f32[32,512]{1,0:T(8,128)S(1)}, u32[]{:S(2)}, u32[]{:S(2)}) collective-permute-start(f32[32,512]{1,0:T(8,128)S(1)} %slice_add_fusion.3), channel_id=1, source_target_pairs={{0,8},{1,9},{2,10},{3,11},{4,12},{5,13},{6,14},{7,15},{8,0},{9,1},... | collective-permute-start | bytes 196616 | tf_op jit(solution)/shard_map/ppermute | solution.py:64
  24.0 5.3 %collective-permute-start.13 = (f32[32,512]{1,0:T(8,128)S(1)}, f32[32,512]{1,0:T(8,128)S(1)}, u32[]{:S(2)}, u32[]{:S(2)}) collective-permute-start(f32[32,512]{1,0:T(8,128)S(1)} %add.38), channel_id=1, source_target_pairs={{0,8},{1,9},{2,10},{3,11},{4,12},{5,13},{6,14},{7,15},{8,0},{9,1},... | collective-permute-start | bytes 196616 | tf_op jit(solution)/shard_map/ppermute | solution.py:64
  26.1 5.5 %collective-permute-start.4 = (f32[32,512]{1,0:T(8,128)S(1)}, f32[32,512]{1,0:T(8,128)S(1)}, u32[]{:S(2)}, u32[]{:S(2)}) collective-permute-start(f32[32,512]{1,0:T(8,128)S(1)} %add.33), channel_id=1, source_target_pairs={{0,16},{1,17},{2,18},{3,19},{4,20},{5,21},{6,22},{7,23},{8,24},{9,... | collective-permute-start | bytes 196616 | tf_op jit(solution)/shard_map/ppermute | solution.py:64
  29.3 4.8 %collective-permute-start.14 = (f32[32,512]{1,0:T(8,128)S(1)}, f32[32,512]{1,0:T(8,128)S(1)}, u32[]{:S(2)}, u32[]{:S(2)}) collective-permute-start(f32[32,512]{1,0:T(8,128)S(1)} %add.39), channel_id=1, source_target_pairs={{0,2},{1,5},{2,0},{3,7},{4,6},{5,1},{6,4},{7,3},{8,10},{9,13},{10,... | collective-permute-start | bytes 196616 | tf_op jit(solution)/shard_map/ppermute | solution.py:64
  31.6 4.3 %collective-permute-start.5 = (f32[32,512]{1,0:T(8,128)S(1)}, f32[32,512]{1,0:T(8,128)S(1)}, u32[]{:S(2)}, u32[]{:S(2)}) collective-permute-start(f32[32,512]{1,0:T(8,128)S(1)} %add.34), channel_id=1, source_target_pairs={{0,2},{1,5},{2,0},{3,7},{4,6},{5,1},{6,4},{7,3},{8,10},{9,13},{10,... | collective-permute-start | bytes 196616 | tf_op jit(solution)/shard_map/ppermute | solution.py:64
  34.1 5.0 %collective-permute-start.15 = (f32[64,512]{1,0:T(8,128)S(1)}, f32[64,512]{1,0:T(8,128)S(1)}, u32[]{:S(2)}, u32[]{:S(2)}) collective-permute-start(f32[64,512]{1,0:T(8,128)S(1)} %pad_maximum_fusion.1.rest_4_), channel_id=1, source_target_pairs={{0,4},{1,3},{2,6},{3,1},{4,0},{5,7},{6,2},{7,5},{8,12},{9,11},{10,... | collective-permute-start | bytes 393224 | tf_op jit(solution)/shard_map/ppermute | solution.py:64
  35.9 5.0 %collective-permute-start.6 = (f32[64,512]{1,0:T(8,128)S(1)}, f32[64,512]{1,0:T(8,128)S(1)}, u32[]{:S(2)}, u32[]{:S(2)}) collective-permute-start(f32[64,512]{1,0:T(8,128)S(1)} %pad_maximum_fusion.rest_0_), channel_id=1, source_target_pairs={{0,4},{1,3},{2,6},{3,1},{4,0},{5,7},{6,2},{7,5},{8,12},{9,11},{10,... | collective-permute-start | bytes 393224 | tf_op jit(solution)/shard_map/ppermute | solution.py:64
  37.5 3.6 %collective-permute-start.16 = (f32[64,512]{1,0:T(8,128)S(1)}, f32[64,512]{1,0:T(8,128)S(1)}, u32[]{:S(2)}, u32[]{:S(2)}) collective-permute-start(f32[64,512]{1,0:T(8,128)S(1)} %pad_maximum_fusion.1.rest_4_), channel_id=1, source_target_pairs={{0,1},{1,0},{2,3},{3,2},{4,5},{5,4},{6,7},{7,6},{8,9},{9,8},{10,11... | collective-permute-start | bytes 393224 | tf_op jit(solution)/shard_map/ppermute | solution.py:64
  37.5 3.6 %collective-permute-start.7 = (f32[64,512]{1,0:T(8,128)S(1)}, f32[64,512]{1,0:T(8,128)S(1)}, u32[]{:S(2)}, u32[]{:S(2)}) collective-permute-start(f32[64,512]{1,0:T(8,128)S(1)} %pad_maximum_fusion.rest_0_), channel_id=1, source_target_pairs={{0,1},{1,0},{2,3},{3,2},{4,5},{5,4},{6,7},{7,6},{8,9},{9,8},{10,11... | collective-permute-start | bytes 393224 | tf_op jit(solution)/shard_map/ppermute | solution.py:64
  39.2 2.0 %collective-permute-start.17 = (f32[64,512]{1,0:T(8,128)S(1)}, f32[64,512]{1,0:T(8,128)S(1)}, u32[]{:S(2)}, u32[]{:S(2)}) collective-permute-start(f32[64,512]{1,0:T(8,128)S(1)} %collective-permute-done.15.rest_5_), channel_id=1, source_target_pairs={{0,1},{1,0},{2,3},{3,2},{4,5},{5,4},{6,7},{7,6},{8,9},{9,8},{10,11... | collective-permute-start | bytes 393224 | tf_op jit(solution)/shard_map/ppermute | solution.py:64
  40.9 1.3 %collective-permute-start.8 = (f32[64,512]{1,0:T(8,128)S(1)}, f32[64,512]{1,0:T(8,128)S(1)}, u32[]{:S(2)}, u32[]{:S(2)}) collective-permute-start(f32[64,512]{1,0:T(8,128)S(1)} %collective-permute-done.6.rest_1_), channel_id=1, source_target_pairs={{0,1},{1,0},{2,3},{3,2},{4,5},{5,4},{6,7},{7,6},{8,9},{9,8},{10,11... | collective-permute-start | bytes 393224 | tf_op jit(solution)/shard_map/ppermute | solution.py:64

commit v5 on v4

--- a/solution.py
+++ b/solution.py
@@ -217,22 +217,30 @@
         value = [split(v * v) for v in value]
         return [product(v, (high, low), NN) for v in value]
 
-    def orthonormal(term, current):
+    def orthonormal(term, first):
         moment = over_chunks(term)
         norm = sum(jnp.sum(v * v, axis=0, keepdims=True) for v in moment)
         norm = jnp.sum(norm, axis=1, keepdims=True)
         scale = topics * jnp.sqrt(norm / (topics * topics) + EPS)
         start = SHIFT / (SHIFT + 1.0)
         weight = 1.0 / ((SHIFT + 1.0) * scale)
-        for v, rows in zip(moment, blocks):
-            value = v * weight + start * current(rows)
-            basis[rows, :] = value
-            basis_high[rows, :], basis_low[rows, :] = split(value)
-        both = (basis_high[...], basis_low[...])
-        cross = dot(both[0], both[1], NT)
-        gram = dot(both[0], both[0], NT) + (cross + cross.T)
-        gram = [gram[rows, :] for rows in blocks]
-        diff = [diagonal(rows, start * start) - g for g, rows in zip(gram, blocks)]
+        if first:
+            for v, rows in zip(moment, blocks):
+                basis[rows, :] = v
+                basis_high[rows, :] = v.astype(BF16)
+            both = (basis_high[...],)
+            both_ways = basis[...] + basis[...].T
+            gram = (start * weight) * both_ways + (weight * weight) * dot(both[0], both[0], NT)
+            diff = [-gram[rows, :] for rows in blocks]
+        else:
+            for v, rows in zip(moment, blocks):
+                value = v * weight + start * basis[rows, :]
+                basis[rows, :] = value
+                basis_high[rows, :], basis_low[rows, :] = split(value)
+            both = (basis_high[...], basis_low[...])
+            cross = dot(both[0], both[1], NT)
+            gram = dot(both[0], both[0], NT) + (cross + cross.T)
+            diff = [diagonal(rows, start * start) - gram[rows, :] for rows in blocks]
         e = 1.0 - start * start
         q = 1.0
         for pair in range(SWEEPS // 2):
@@ -266,15 +274,22 @@
                 e, c1, c2, c3 = following(e)
                 diff = [c1 * diff[k] + c2 * second[k] + c3 * third[k] for k in each]
         parts = [split(f) for f in factor]
-        value = [q * basis[rows, :] + product(parts[k], both, NN) for k, rows in enumerate(blocks)]
+        if first:
+            value = [dot(parts[k][0], both[0], NN) + dot(parts[k][1], both[0], NN) for k in each]
+            value = [
+                weight * (value[k] + q * basis[rows, :]) + (start * factor[k] + diagonal(rows, q * start))
+                for k, rows in enumerate(blocks)
+            ]
+        else:
+            value = [q * basis[rows, :] + product(parts[k], both, NN) for k, rows in enumerate(blocks)]
         for v, rows in zip(value, blocks):
             basis[rows, :] = v
             basis_high[rows, :], basis_low[rows, :] = split(v)
 
-    orthonormal(picked, lambda rows: diagonal(rows, 1.0))
+    orthonormal(picked, True)
 
     for _ in range(ITERS):
-        orthonormal(moments, lambda rows: basis[rows, :])
+        orthonormal(moments, False)
     parts = (basis_high[...], basis_low[...])
     total = jnp.zeros((1, topics), F32)
     for r in range(0, docs, chunk):

time: 61 us -> 60.1 us (0.985)
  Pallas kernels: 23.6 us -> 22.6 us
    pallas_call x1, Pallas kernels: 18.5 us -> 17.6 us  [iterate(): pl.pallas_call(functools.partial(iterate_kernel, chunk, pairs, CHAINS), i...]
where the time goes in v5:
time: 60.1 us; the launch traced here: 59.9 us
  starting transfers between devices  24.1 us (40%)
  Pallas kernels  22.6 us (38%)
  waiting for transfers between devices  11.4 us (19%)
  local copies, waits for them, and re-layouts  0.85 us (1%)
  between operations  0.77 us (1%)
    ppermute x18, starting transfers between devices, exchange(): return lax.ppermute(value, AXES, perm)  24.1 us
    pallas_call x1, Pallas kernels, iterate(): pl.pallas_call(functools.partial(iterate_kernel, chunk, pairs, CHAINS), i...  17.6 us
    ppermute x18, waiting for transfers between devices, exchange(): return lax.ppermute(value, AXES, perm)  11.4 us
    pallas_call x1, Pallas kernels, partial_rows(): pl.pallas_call(functools.partial(whiten_kernel, pairs, unit_blocks, half_...  5.01 us
  transfers between devices with their start and end apart: 18, of which 11 were waited for; matrix products, arithmetic and copies ran while one was open for 1% of the time, Pallas kernels for 0%

profile of v5, /device:TPU:0, one launch (start us, length us, event | category | flops | bytes accessed | tf_op | source)
XLA Modules:
  0.0 59.9 jit_solution(7775617600308521957)
XLA Ops:
  0.6 0.7 %copy-done = s32[1,32,2]{1,2,0:T(2,128)S(1)} copy-done((s32[1,32,2]{1,2,0:T(2,128)S(1)}, s32[1,32,2]{1,2,0:T(2,128)}, u32[]{:S(2)}) %copy-start) | copy-done | bytes 280
  1.3 5.0 %whiten.1 = (f32[128,512]{1,0:T(8,128)S(1)}, f32[128,512]{1,0:T(8,128)S(1)}, f32[128,512]{1,0:T(8,128)S(1)}, f32[128,512]{1,0:T(8,128)}) custom-call(s32[2,32]{1,0:T(2,128)S(1)} %bitcast.6, s32[32,2,16,128]{3,2,1,0:T(8,128)} %bitcast.7, bf16[4096,512]{1,0:T(8,128)(2,1)} %table.1), custom_call_target="tpu_custom_call" | custom-call | tf_op jit(solution)/shard_map/whiten/pallas_call | solution.py:131
  6.3 0.5 collective-permute-start.9
  6.9 0.1 collective-permute-start
  6.9 1.3 %collective-permute-done.9 = f32[128,512]{1,0:T(8,128)S(1)} collective-permute-done((f32[128,512]{1,0:T(8,128)}, f32[128,512]{1,0:T(8,128)S(1)}, u32[]{:S(2)}, u32[]{:S(2)}) %collective-permute-start.9) | collective-permute-done | bytes 262176 | tf_op jit(solution)/shard_map/ppermute | solution.py:64
  8.3 2.9 %collective-permute-start.10 = (f32[64,512]{1,0:T(8,128)S(1)}, f32[64,512]{1,0:T(8,128)S(1)}, u32[]{:S(2)}, u32[]{:S(2)}) collective-permute-start(f32[64,512]{1,0:T(8,128)S(1)} %slice.37), channel_id=1, source_target_pairs={{0,4},{1,3},{2,6},{3,1},{4,0},{5,7},{6,2},{7,5},{8,12},{9,11},{10,... | collective-permute-start | bytes 393224 | tf_op jit(solution)/shard_map/ppermute | solution.py:64
  11.2 0.0 collective-permute-done
  11.3 0.1 collective-permute-start.1
  11.4 2.8 %collective-permute-done.10 = f32[64,512]{1,0:T(8,128)S(1)} collective-permute-done((f32[64,512]{1,0:T(8,128)S(1)}, f32[64,512]{1,0:T(8,128)S(1)}, u32[]{:S(2)}, u32[]{:S(2)}) %collective-permute-start.10) | collective-permute-done | bytes 131104 | tf_op jit(solution)/shard_map/ppermute | solution.py:64
  14.2 2.1 %collective-permute-start.11 = (f32[32,512]{1,0:T(8,128)S(1)}, f32[32,512]{1,0:T(8,128)S(1)}, u32[]{:S(2)}, u32[]{:S(2)}) collective-permute-start(f32[32,512]{1,0:T(8,128)S(1)} %slice.39), channel_id=1, source_target_pairs={{0,2},{1,5},{2,0},{3,7},{4,6},{5,1},{6,4},{7,3},{8,10},{9,13},{10,... | collective-permute-start | bytes 196616 | tf_op jit(solution)/shard_map/ppermute | solution.py:64
  16.3 1.6 %collective-permute-start.2 = (f32[32,512]{1,0:T(8,128)S(1)}, f32[32,512]{1,0:T(8,128)S(1)}, u32[]{:S(2)}, u32[]{:S(2)}) collective-permute-start(f32[32,512]{1,0:T(8,128)S(1)} %slice.35), channel_id=1, source_target_pairs={{0,2},{1,5},{2,0},{3,7},{4,6},{5,1},{6,4},{7,3},{8,10},{9,13},{10,... | collective-permute-start | bytes 196616 | tf_op jit(solution)/shard_map/ppermute | solution.py:64
  17.9 0.6 %collective-permute-done.11 = f32[32,512]{1,0:T(8,128)S(1)} collective-permute-done((f32[32,512]{1,0:T(8,128)S(1)}, f32[32,512]{1,0:T(8,128)S(1)}, u32[]{:S(2)}, u32[]{:S(2)}) %collective-permute-start.11) | collective-permute-done | bytes 65568 | tf_op jit(solution)/shard_map/ppermute | solution.py:64
  18.6 3.2 %collective-permute-start.12 = (f32[32,512]{1,0:T(8,128)S(1)}, f32[32,512]{1,0:T(8,128)S(1)}, u32[]{:S(2)}, u32[]{:S(2)}) collective-permute-start(f32[32,512]{1,0:T(8,128)S(1)} %slice_add_fusion.2), channel_id=1, source_target_pairs={{0,16},{1,17},{2,18},{3,19},{4,20},{5,21},{6,22},{7,23},{8,24},{9,... | collective-permute-start | bytes 196616 | tf_op jit(solution)/shard_map/ppermute | solution.py:64
  21.7 0.0 collective-permute-done.2
  21.7 1.6 %collective-permute-start.3 = (f32[32,512]{1,0:T(8,128)S(1)}, f32[32,512]{1,0:T(8,128)S(1)}, u32[]{:S(2)}, u32[]{:S(2)}) collective-permute-start(f32[32,512]{1,0:T(8,128)S(1)} %slice_add_fusion.3), channel_id=1, source_target_pairs={{0,8},{1,9},{2,10},{3,11},{4,12},{5,13},{6,14},{7,15},{8,0},{9,1},... | collective-permute-start | bytes 196616 | tf_op jit(solution)/shard_map/ppermute | solution.py:64
  23.4 0.6 collective-permute-done.12
  24.0 2.0 %collective-permute-start.13 = (f32[32,512]{1,0:T(8,128)S(1)}, f32[32,512]{1,0:T(8,128)S(1)}, u32[]{:S(2)}, u32[]{:S(2)}) collective-permute-start(f32[32,512]{1,0:T(8,128)S(1)} %add.38), channel_id=1, source_target_pairs={{0,8},{1,9},{2,10},{3,11},{4,12},{5,13},{6,14},{7,15},{8,0},{9,1},... | collective-permute-start | bytes 196616 | tf_op jit(solution)/shard_map/ppermute | solution.py:64
  25.9 0.1 collective-permute-done.3
  26.1 3.2 %collective-permute-start.4 = (f32[32,512]{1,0:T(8,128)S(1)}, f32[32,512]{1,0:T(8,128)S(1)}, u32[]{:S(2)}, u32[]{:S(2)}) collective-permute-start(f32[32,512]{1,0:T(8,128)S(1)} %add.33), channel_id=1, source_target_pairs={{0,16},{1,17},{2,18},{3,19},{4,20},{5,21},{6,22},{7,23},{8,24},{9,... | collective-permute-start | bytes 196616 | tf_op jit(solution)/shard_map/ppermute | solution.py:64
  29.3 1.6 %collective-permute-start.14 = (f32[32,512]{1,0:T(8,128)S(1)}, f32[32,512]{1,0:T(8,128)S(1)}, u32[]{:S(2)}, u32[]{:S(2)}) collective-permute-start(f32[32,512]{1,0:T(8,128)S(1)} %add.39), channel_id=1, source_target_pairs={{0,2},{1,5},{2,0},{3,7},{4,6},{5,1},{6,4},{7,3},{8,10},{9,13},{10,... | collective-permute-start | bytes 196616 | tf_op jit(solution)/shard_map/ppermute | solution.py:64
  30.9 0.6 %collective-permute-done.4 = f32[32,512]{1,0:T(8,128)S(1)} collective-permute-done((f32[32,512]{1,0:T(8,128)S(1)}, f32[32,512]{1,0:T(8,128)S(1)}, u32[]{:S(2)}, u32[]{:S(2)}) %collective-permute-start.4) | collective-permute-done | bytes 65568 | tf_op jit(solution)/shard_map/ppermute | solution.py:64
  31.6 1.6 %collective-permute-start.5 = (f32[32,512]{1,0:T(8,128)S(1)}, f32[32,512]{1,0:T(8,128)S(1)}, u32[]{:S(2)}, u32[]{:S(2)}) collective-permute-start(f32[32,512]{1,0:T(8,128)S(1)} %add.34), channel_id=1, source_target_pairs={{0,2},{1,5},{2,0},{3,7},{4,6},{5,1},{6,4},{7,3},{8,10},{9,13},{10,... | collective-permute-start | bytes 196616 | tf_op jit(solution)/shard_map/ppermute | solution.py:64
  33.2 1.0 %collective-permute-done.14 = f32[32,512]{1,0:T(8,128)S(1)} collective-permute-done((f32[32,512]{1,0:T(8,128)S(1)}, f32[32,512]{1,0:T(8,128)S(1)}, u32[]{:S(2)}, u32[]{:S(2)}) %collective-permute-start.14) | collective-permute-done | bytes 65568 | tf_op jit(solution)/shard_map/ppermute | solution.py:64
  34.1 1.6 %collective-permute-start.15 = (f32[64,512]{1,0:T(8,128)S(1)}, f32[64,512]{1,0:T(8,128)S(1)}, u32[]{:S(2)}, u32[]{:S(2)}) collective-permute-start(f32[64,512]{1,0:T(8,128)S(1)} %pad_maximum_fusion.1.rest_4_), channel_id=1, source_target_pairs={{0,4},{1,3},{2,6},{3,1},{4,0},{5,7},{6,2},{7,5},{8,12},{9,11},{10,... | collective-permute-start | bytes 393224 | tf_op jit(solution)/shard_map/ppermute | solution.py:64
  35.7 0.2 collective-permute-done.5
  35.9 1.6 %collective-permute-start.6 = (f32[64,512]{1,0:T(8,128)S(1)}, f32[64,512]{1,0:T(8,128)S(1)}, u32[]{:S(2)}, u32[]{:S(2)}) collective-permute-start(f32[64,512]{1,0:T(8,128)S(1)} %pad_maximum_fusion.rest_0_), channel_id=1, source_target_pairs={{0,4},{1,3},{2,6},{3,1},{4,0},{5,7},{6,2},{7,5},{8,12},{9,11},{10,... | collective-permute-start | bytes 393224 | tf_op jit(solution)/shard_map/ppermute | solution.py:64
  37.5 0.5 collective-permute-start.7
  38.0 1.2 %collective-permute-done.15.rest_5_ = f32[64,512]{1,0:T(8,128)S(1)} collective-permute-done((f32[64,512]{1,0:T(8,128)S(1)}, f32[64,512]{1,0:T(8,128)S(1)}, u32[]{:S(2)}, u32[]{:S(2)}) %collective-permute-start.15) | collective-permute-done | bytes 131104 | tf_op jit(solution)/shard_map/ppermute | solution.py:64
  39.2 1.8 %collective-permute-done.6.rest_1_ = f32[64,512]{1,0:T(8,128)S(1)} collective-permute-done((f32[64,512]{1,0:T(8,128)S(1)}, f32[64,512]{1,0:T(8,128)S(1)}, u32[]{:S(2)}, u32[]{:S(2)}) %collective-permute-start.6) | collective-permute-done | bytes 131104 | tf_op jit(solution)/shard_map/ppermute | solution.py:64
  41.0 0.1 copy.6.seeds_ref
  41.1 1.2 %collective-permute-done.8.rest_3_ = f32[64,512]{1,0:T(8,128)S(1)} collective-permute-done((f32[64,512]{1,0:T(8,128)S(1)}, f32[64,512]{1,0:T(8,128)S(1)}, u32[]{:S(2)}, u32[]{:S(2)}) %collective-permute-start.8) | collective-permute-done | bytes 131104 | tf_op jit(solution)/shard_map/ppermute | solution.py:64
  42.3 17.6 %iterate.1 = (f32[128,512]{1,0:T(8,128)}, f32[1,512]{1,0:T(1,128)}) custom-call(s32[512,1]{1,0:T(8,128)S(1)} %copy.6.seeds_ref, f32[64,512]{1,0:T(8,128)S(1)} %pad_maximum_fusion.rest_0_, f32[64,512]{1,0:T(8,128)S(1)} %collective-permute-done.6.rest_1_, f32[64,512]{1,0:T(8,128)S(1)} %collective-permute-done.7.rest_2_, ...), custom_call_target="tpu_custom_call" | custom-call | tf_op jit(solution)/shard_map/iterate/pallas_call | solution.py:308
  (27 shorter events, 0.3 us)
Async XLA Ops:
  0.6 0.7 %copy-start = (s32[1,32,2]{1,2,0:T(2,128)S(1)}, s32[1,32,2]{1,2,0:T(2,128)}, u32[]{:S(2)}) copy-start(s32[1,32,2]{1,2,0:T(2,128)} %param.5) | copy-start | bytes 772
  1.3 39.6 %copy-start.1 = (s32[512]{0:T(512)S(1)}, s32[512]{0:T(512)}, u32[]{:S(2)}) copy-start(s32[512]{0:T(512)} %param.7) | copy-start | bytes 6148
  6.3 1.9 %collective-permute-start.9 = (f32[128,512]{1,0:T(8,128)}, f32[128,512]{1,0:T(8,128)S(1)}, u32[]{:S(2)}, u32[]{:S(2)}) collective-permute-start(f32[128,512]{1,0:T(8,128)} %get-tuple-element.11), channel_id=1, source_target_pairs={{0,1},{1,0},{2,3},{3,2},{4,5},{5,4},{6,7},{7,6},{8,9},{9,8},{10,11... | collective-permute-start | bytes 786440 | tf_op jit(solution)/shard_map/ppermute | solution.py:64
  6.9 4.4 %collective-permute-start = (f32[128,512]{1,0:T(8,128)S(1)}, f32[128,512]{1,0:T(8,128)S(1)}, u32[]{:S(2)}, u32[]{:S(2)}) collective-permute-start(f32[128,512]{1,0:T(8,128)S(1)} %get-tuple-element.9), channel_id=1, source_target_pairs={{0,1},{1,0},{2,3},{3,2},{4,5},{5,4},{6,7},{7,6},{8,9},{9,8},{10,11... | collective-permute-start | bytes 786440 | tf_op jit(solution)/shard_map/ppermute | solution.py:64
  8.3 5.9 %collective-permute-start.10 = (f32[64,512]{1,0:T(8,128)S(1)}, f32[64,512]{1,0:T(8,128)S(1)}, u32[]{:S(2)}, u32[]{:S(2)}) collective-permute-start(f32[64,512]{1,0:T(8,128)S(1)} %slice.37), channel_id=1, source_target_pairs={{0,4},{1,3},{2,6},{3,1},{4,0},{5,7},{6,2},{7,5},{8,12},{9,11},{10,... | collective-permute-start | bytes 393224 | tf_op jit(solution)/shard_map/ppermute | solution.py:64
  11.3 5.0 %collective-permute-start.1 = (f32[64,512]{1,0:T(8,128)S(1)}, f32[64,512]{1,0:T(8,128)S(1)}, u32[]{:S(2)}, u32[]{:S(2)}) collective-permute-start(f32[64,512]{1,0:T(8,128)S(1)} %slice.33), channel_id=1, source_target_pairs={{0,4},{1,3},{2,6},{3,1},{4,0},{5,7},{6,2},{7,5},{8,12},{9,11},{10,... | collective-permute-start | bytes 393224 | tf_op jit(solution)/shard_map/ppermute | solution.py:64
  14.2 4.4 %collective-permute-start.11 = (f32[32,512]{1,0:T(8,128)S(1)}, f32[32,512]{1,0:T(8,128)S(1)}, u32[]{:S(2)}, u32[]{:S(2)}) collective-permute-start(f32[32,512]{1,0:T(8,128)S(1)} %slice.39), channel_id=1, source_target_pairs={{0,2},{1,5},{2,0},{3,7},{4,6},{5,1},{6,4},{7,3},{8,10},{9,13},{10,... | collective-permute-start | bytes 196616 | tf_op jit(solution)/shard_map/ppermute | solution.py:64
  16.3 5.4 %collective-permute-start.2 = (f32[32,512]{1,0:T(8,128)S(1)}, f32[32,512]{1,0:T(8,128)S(1)}, u32[]{:S(2)}, u32[]{:S(2)}) collective-permute-start(f32[32,512]{1,0:T(8,128)S(1)} %slice.35), channel_id=1, source_target_pairs={{0,2},{1,5},{2,0},{3,7},{4,6},{5,1},{6,4},{7,3},{8,10},{9,13},{10,... | collective-permute-start | bytes 196616 | tf_op jit(solution)/shard_map/ppermute | solution.py:64
  18.6 5.4 %collective-permute-start.12 = (f32[32,512]{1,0:T(8,128)S(1)}, f32[32,512]{1,0:T(8,128)S(1)}, u32[]{:S(2)}, u32[]{:S(2)}) collective-permute-start(f32[32,512]{1,0:T(8,128)S(1)} %slice_add_fusion.2), channel_id=1, source_target_pairs={{0,16},{1,17},{2,18},{3,19},{4,20},{5,21},{6,22},{7,23},{8,24},{9,... | collective-permute-start | bytes 196616 | tf_op jit(solution)/shard_map/ppermute | solution.py:64
  21.7 4.3 %collective-permute-start.3 = (f32[32,512]{1,0:T(8,128)S(1)}, f32[32,512]{1,0:T(8,128)S(1)}, u32[]{:S(2)}, u32[]{:S(2)}) collective-permute-start(f32[32,512]{1,0:T(8,128)S(1)} %slice_add_fusion.3), channel_id=1, source_target_pairs={{0,8},{1,9},{2,10},{3,11},{4,12},{5,13},{6,14},{7,15},{8,0},{9,1},... | collective-permute-start | bytes 196616 | tf_op jit(solution)/shard_map/ppermute | solution.py:64
  24.0 5.3 %collective-permute-start.13 = (f32[32,512]{1,0:T(8,128)S(1)}, f32[32,512]{1,0:T(8,128)S(1)}, u32[]{:S(2)}, u32[]{:S(2)}) collective-permute-start(f32[32,512]{1,0:T(8,128)S(1)} %add.38), channel_id=1, source_target_pairs={{0,8},{1,9},{2,10},{3,11},{4,12},{5,13},{6,14},{7,15},{8,0},{9,1},... | collective-permute-start | bytes 196616 | tf_op jit(solution)/shard_map/ppermute | solution.py:64
  26.1 5.5 %collective-permute-start.4 = (f32[32,512]{1,0:T(8,128)S(1)}, f32[32,512]{1,0:T(8,128)S(1)}, u32[]{:S(2)}, u32[]{:S(2)}) collective-permute-start(f32[32,512]{1,0:T(8,128)S(1)} %add.33), channel_id=1, source_target_pairs={{0,16},{1,17},{2,18},{3,19},{4,20},{5,21},{6,22},{7,23},{8,24},{9,... | collective-permute-start | bytes 196616 | tf_op jit(solution)/shard_map/ppermute | solution.py:64
  29.3 4.8 %collective-permute-start.14 = (f32[32,512]{1,0:T(8,128)S(1)}, f32[32,512]{1,0:T(8,128)S(1)}, u32[]{:S(2)}, u32[]{:S(2)}) collective-permute-start(f32[32,512]{1,0:T(8,128)S(1)} %add.39), channel_id=1, source_target_pairs={{0,2},{1,5},{2,0},{3,7},{4,6},{5,1},{6,4},{7,3},{8,10},{9,13},{10,... | collective-permute-start | bytes 196616 | tf_op jit(solution)/shard_map/ppermute | solution.py:64
  31.6 4.3 %collective-permute-start.5 = (f32[32,512]{1,0:T(8,128)S(1)}, f32[32,512]{1,0:T(8,128)S(1)}, u32[]{:S(2)}, u32[]{:S(2)}) collective-permute-start(f32[32,512]{1,0:T(8,128)S(1)} %add.34), channel_id=1, source_target_pairs={{0,2},{1,5},{2,0},{3,7},{4,6},{5,1},{6,4},{7,3},{8,10},{9,13},{10,... | collective-permute-start | bytes 196616 | tf_op jit(solution)/shard_map/ppermute | solution.py:64
  34.1 5.0 %collective-permute-start.15 = (f32[64,512]{1,0:T(8,128)S(1)}, f32[64,512]{1,0:T(8,128)S(1)}, u32[]{:S(2)}, u32[]{:S(2)}) collective-permute-start(f32[64,512]{1,0:T(8,128)S(1)} %pad_maximum_fusion.1.rest_4_), channel_id=1, source_target_pairs={{0,4},{1,3},{2,6},{3,1},{4,0},{5,7},{6,2},{7,5},{8,12},{9,11},{10,... | collective-permute-start | bytes 393224 | tf_op jit(solution)/shard_map/ppermute | solution.py:64
  35.9 5.0 %collective-permute-start.6 = (f32[64,512]{1,0:T(8,128)S(1)}, f32[64,512]{1,0:T(8,128)S(1)}, u32[]{:S(2)}, u32[]{:S(2)}) collective-permute-start(f32[64,512]{1,0:T(8,128)S(1)} %pad_maximum_fusion.rest_0_), channel_id=1, source_target_pairs={{0,4},{1,3},{2,6},{3,1},{4,0},{5,7},{6,2},{7,5},{8,12},{9,11},{10,... | collective-permute-start | bytes 393224 | tf_op jit(solution)/shard_map/ppermute | solution.py:64
  37.5 3.6 %collective-permute-start.16 = (f32[64,512]{1,0:T(8,128)S(1)}, f32[64,512]{1,0:T(8,128)S(1)}, u32[]{:S(2)}, u32[]{:S(2)}) collective-permute-start(f32[64,512]{1,0:T(8,128)S(1)} %pad_maximum_fusion.1.rest_4_), channel_id=1, source_target_pairs={{0,1},{1,0},{2,3},{3,2},{4,5},{5,4},{6,7},{7,6},{8,9},{9,8},{10,11... | collective-permute-start | bytes 393224 | tf_op jit(solution)/shard_map/ppermute | solution.py:64
  37.5 3.6 %collective-permute-start.7 = (f32[64,512]{1,0:T(8,128)S(1)}, f32[64,512]{1,0:T(8,128)S(1)}, u32[]{:S(2)}, u32[]{:S(2)}) collective-permute-start(f32[64,512]{1,0:T(8,128)S(1)} %pad_maximum_fusion.rest_0_), channel_id=1, source_target_pairs={{0,1},{1,0},{2,3},{3,2},{4,5},{5,4},{6,7},{7,6},{8,9},{9,8},{10,11... | collective-permute-start | bytes 393224 | tf_op jit(solution)/shard_map/ppermute | solution.py:64
  39.2 2.0 %collective-permute-start.17 = (f32[64,512]{1,0:T(8,128)S(1)}, f32[64,512]{1,0:T(8,128)S(1)}, u32[]{:S(2)}, u32[]{:S(2)}) collective-permute-start(f32[64,512]{1,0:T(8,128)S(1)} %collective-permute-done.15.rest_5_), channel_id=1, source_target_pairs={{0,1},{1,0},{2,3},{3,2},{4,5},{5,4},{6,7},{7,6},{8,9},{9,8},{10,11... | collective-permute-start | bytes 393224 | tf_op jit(solution)/shard_map/ppermute | solution.py:64
  40.9 1.3 %collective-permute-start.8 = (f32[64,512]{1,0:T(8,128)S(1)}, f32[64,512]{1,0:T(8,128)S(1)}, u32[]{:S(2)}, u32[]{:S(2)}) collective-permute-start(f32[64,512]{1,0:T(8,128)S(1)} %collective-permute-done.6.rest_1_), channel_id=1, source_target_pairs={{0,1},{1,0},{2,3},{3,2},{4,5},{5,4},{6,7},{7,6},{8,9},{9,8},{10,11... | collective-permute-start | bytes 393224 | tf_op jit(solution)/shard_map/ppermute | solution.py:64

commit v6 on v5

--- a/solution.py
+++ b/solution.py
@@ -229,7 +229,7 @@
                 basis[rows, :] = v
                 basis_high[rows, :] = v.astype(BF16)
             both = (basis_high[...],)
-            both_ways = basis[...] + basis[...].T
+            both_ways = basis[...] + both[0].T.astype(F32)
             gram = (start * weight) * both_ways + (weight * weight) * dot(both[0], both[0], NT)
             diff = [-gram[rows, :] for rows in blocks]
         else:
@@ -238,8 +238,8 @@
                 basis[rows, :] = value
                 basis_high[rows, :], basis_low[rows, :] = split(value)
             both = (basis_high[...], basis_low[...])
-            cross = dot(both[0], both[1], NT)
-            gram = dot(both[0], both[0], NT) + (cross + cross.T)
+            cross = dot(both[0], both[1], NT).astype(BF16)
+            gram = dot(both[0], both[0], NT) + (cross.astype(F32) + cross.T.astype(F32))
             diff = [diagonal(rows, start * start) - gram[rows, :] for rows in blocks]
         e = 1.0 - start * start
         q = 1.0
@@ -296,9 +296,13 @@
         value = product((white_high[r : r + chunk, :], white_low[r : r + chunk, :]), parts, NT)
         total += jnp.sum(value * value * value, axis=0, keepdims=True)
     weights_ref[...] = total / docs
-    basis[...] = basis[...].T * math.sqrt(topics)
     own_rows = own_out.shape[0]
-    own_out[...] = basis[pl.ds(pl.multiple_of(lax.axis_index("vocab") * own_rows, own_rows), own_rows), :]
+    own = pl.ds(pl.multiple_of(lax.axis_index("vocab") * own_rows, own_rows), own_rows)
+    if own_rows % 128 == 0:
+        own_out[...] = basis[:, own].T * math.sqrt(topics)
+    else:
+        basis[...] = basis[...].T * math.sqrt(topics)
+        own_out[...] = basis[own, :]
 
 
 def iterate(pieces, seeds, docs, pairs, own_rows):

time: 60.1 us -> 60 us (level)
  no operation moved by 1% of the time
where the time goes in v6:
time: 60 us; the launch traced here: 59.8 us
  starting transfers between devices  24.1 us (40%)
  Pallas kernels  22.5 us (38%)
  waiting for transfers between devices  11.4 us (19%)
  local copies, waits for them, and re-layouts  0.85 us (1%)
  between operations  0.77 us (1%)
    ppermute x18, starting transfers between devices, exchange(): return lax.ppermute(value, AXES, perm)  24.1 us
    pallas_call x1, Pallas kernels, iterate(): pl.pallas_call(functools.partial(iterate_kernel, chunk, pairs, CHAINS), i...  17.5 us
    ppermute x18, waiting for transfers between devices, exchange(): return lax.ppermute(value, AXES, perm)  11.4 us
    pallas_call x1, Pallas kernels, partial_rows(): pl.pallas_call(functools.partial(whiten_kernel, pairs, unit_blocks, half_...  5.01 us
  transfers between devices with their start and end apart: 18, of which 11 were waited for; matrix products, arithmetic and copies ran while one was open for 1% of the time, Pallas kernels for 0%

profile of v6, /device:TPU:0, one launch (start us, length us, event | category | flops | bytes accessed | tf_op | source)
XLA Modules:
  0.0 59.8 jit_solution(4148054473000951236)
XLA Ops:
  0.6 0.7 %copy-done = s32[1,32,2]{1,2,0:T(2,128)S(1)} copy-done((s32[1,32,2]{1,2,0:T(2,128)S(1)}, s32[1,32,2]{1,2,0:T(2,128)}, u32[]{:S(2)}) %copy-start) | copy-done | bytes 280
  1.3 5.0 %whiten.1 = (f32[128,512]{1,0:T(8,128)S(1)}, f32[128,512]{1,0:T(8,128)S(1)}, f32[128,512]{1,0:T(8,128)S(1)}, f32[128,512]{1,0:T(8,128)}) custom-call(s32[2,32]{1,0:T(2,128)S(1)} %bitcast.6, s32[32,2,16,128]{3,2,1,0:T(8,128)} %bitcast.7, bf16[4096,512]{1,0:T(8,128)(2,1)} %table.1), custom_call_target="tpu_custom_call" | custom-call | tf_op jit(solution)/shard_map/whiten/pallas_call | solution.py:131
  6.3 0.5 collective-permute-start.9
  6.8 0.1 collective-permute-start
  6.9 1.3 %collective-permute-done.9 = f32[128,512]{1,0:T(8,128)S(1)} collective-permute-done((f32[128,512]{1,0:T(8,128)}, f32[128,512]{1,0:T(8,128)S(1)}, u32[]{:S(2)}, u32[]{:S(2)}) %collective-permute-start.9) | collective-permute-done | bytes 262176 | tf_op jit(solution)/shard_map/ppermute | solution.py:64
  8.3 2.9 %collective-permute-start.10 = (f32[64,512]{1,0:T(8,128)S(1)}, f32[64,512]{1,0:T(8,128)S(1)}, u32[]{:S(2)}, u32[]{:S(2)}) collective-permute-start(f32[64,512]{1,0:T(8,128)S(1)} %slice.37), channel_id=1, source_target_pairs={{0,4},{1,3},{2,6},{3,1},{4,0},{5,7},{6,2},{7,5},{8,12},{9,11},{10,... | collective-permute-start | bytes 393224 | tf_op jit(solution)/shard_map/ppermute | solution.py:64
  11.3 0.1 collective-permute-start.1
  11.4 2.8 %collective-permute-done.10 = f32[64,512]{1,0:T(8,128)S(1)} collective-permute-done((f32[64,512]{1,0:T(8,128)S(1)}, f32[64,512]{1,0:T(8,128)S(1)}, u32[]{:S(2)}, u32[]{:S(2)}) %collective-permute-start.10) | collective-permute-done | bytes 131104 | tf_op jit(solution)/shard_map/ppermute | solution.py:64
  14.2 2.1 %collective-permute-start.11 = (f32[32,512]{1,0:T(8,128)S(1)}, f32[32,512]{1,0:T(8,128)S(1)}, u32[]{:S(2)}, u32[]{:S(2)}) collective-permute-start(f32[32,512]{1,0:T(8,128)S(1)} %slice.39), channel_id=1, source_target_pairs={{0,2},{1,5},{2,0},{3,7},{4,6},{5,1},{6,4},{7,3},{8,10},{9,13},{10,... | collective-permute-start | bytes 196616 | tf_op jit(solution)/shard_map/ppermute | solution.py:64
  16.3 0.0 collective-permute-done.1
  16.3 1.6 %collective-permute-start.2 = (f32[32,512]{1,0:T(8,128)S(1)}, f32[32,512]{1,0:T(8,128)S(1)}, u32[]{:S(2)}, u32[]{:S(2)}) collective-permute-start(f32[32,512]{1,0:T(8,128)S(1)} %slice.35), channel_id=1, source_target_pairs={{0,2},{1,5},{2,0},{3,7},{4,6},{5,1},{6,4},{7,3},{8,10},{9,13},{10,... | collective-permute-start | bytes 196616 | tf_op jit(solution)/shard_map/ppermute | solution.py:64
  17.9 0.6 %collective-permute-done.11 = f32[32,512]{1,0:T(8,128)S(1)} collective-permute-done((f32[32,512]{1,0:T(8,128)S(1)}, f32[32,512]{1,0:T(8,128)S(1)}, u32[]{:S(2)}, u32[]{:S(2)}) %collective-permute-start.11) | collective-permute-done | bytes 65568 | tf_op jit(solution)/shard_map/ppermute | solution.py:64
  18.6 3.2 %collective-permute-start.12 = (f32[32,512]{1,0:T(8,128)S(1)}, f32[32,512]{1,0:T(8,128)S(1)}, u32[]{:S(2)}, u32[]{:S(2)}) collective-permute-start(f32[32,512]{1,0:T(8,128)S(1)} %slice_add_fusion.2), channel_id=1, source_target_pairs={{0,16},{1,17},{2,18},{3,19},{4,20},{5,21},{6,22},{7,23},{8,24},{9,... | collective-permute-start | bytes 196616 | tf_op jit(solution)/shard_map/ppermute | solution.py:64
  21.7 1.6 %collective-permute-start.3 = (f32[32,512]{1,0:T(8,128)S(1)}, f32[32,512]{1,0:T(8,128)S(1)}, u32[]{:S(2)}, u32[]{:S(2)}) collective-permute-start(f32[32,512]{1,0:T(8,128)S(1)} %slice_add_fusion.3), channel_id=1, source_target_pairs={{0,8},{1,9},{2,10},{3,11},{4,12},{5,13},{6,14},{7,15},{8,0},{9,1},... | collective-permute-start | bytes 196616 | tf_op jit(solution)/shard_map/ppermute | solution.py:64
  23.4 0.6 collective-permute-done.12
  24.0 2.0 %collective-permute-start.13 = (f32[32,512]{1,0:T(8,128)S(1)}, f32[32,512]{1,0:T(8,128)S(1)}, u32[]{:S(2)}, u32[]{:S(2)}) collective-permute-start(f32[32,512]{1,0:T(8,128)S(1)} %add.38), channel_id=1, source_target_pairs={{0,8},{1,9},{2,10},{3,11},{4,12},{5,13},{6,14},{7,15},{8,0},{9,1},... | collective-permute-start | bytes 196616 | tf_op jit(solution)/shard_map/ppermute | solution.py:64
  25.9 0.1 collective-permute-done.3
  26.1 3.2 %collective-permute-start.4 = (f32[32,512]{1,0:T(8,128)S(1)}, f32[32,512]{1,0:T(8,128)S(1)}, u32[]{:S(2)}, u32[]{:S(2)}) collective-permute-start(f32[32,512]{1,0:T(8,128)S(1)} %add.33), channel_id=1, source_target_pairs={{0,16},{1,17},{2,18},{3,19},{4,20},{5,21},{6,22},{7,23},{8,24},{9,... | collective-permute-start | bytes 196616 | tf_op jit(solution)/shard_map/ppermute | solution.py:64
  29.3 1.6 %collective-permute-start.14 = (f32[32,512]{1,0:T(8,128)S(1)}, f32[32,512]{1,0:T(8,128)S(1)}, u32[]{:S(2)}, u32[]{:S(2)}) collective-permute-start(f32[32,512]{1,0:T(8,128)S(1)} %add.39), channel_id=1, source_target_pairs={{0,2},{1,5},{2,0},{3,7},{4,6},{5,1},{6,4},{7,3},{8,10},{9,13},{10,... | collective-permute-start | bytes 196616 | tf_op jit(solution)/shard_map/ppermute | solution.py:64
  30.9 0.6 %collective-permute-done.4 = f32[32,512]{1,0:T(8,128)S(1)} collective-permute-done((f32[32,512]{1,0:T(8,128)S(1)}, f32[32,512]{1,0:T(8,128)S(1)}, u32[]{:S(2)}, u32[]{:S(2)}) %collective-permute-start.4) | collective-permute-done | bytes 65568 | tf_op jit(solution)/shard_map/ppermute | solution.py:64
  31.6 1.6 %collective-permute-start.5 = (f32[32,512]{1,0:T(8,128)S(1)}, f32[32,512]{1,0:T(8,128)S(1)}, u32[]{:S(2)}, u32[]{:S(2)}) collective-permute-start(f32[32,512]{1,0:T(8,128)S(1)} %add.34), channel_id=1, source_target_pairs={{0,2},{1,5},{2,0},{3,7},{4,6},{5,1},{6,4},{7,3},{8,10},{9,13},{10,... | collective-permute-start | bytes 196616 | tf_op jit(solution)/shard_map/ppermute | solution.py:64
  33.2 1.0 %collective-permute-done.14 = f32[32,512]{1,0:T(8,128)S(1)} collective-permute-done((f32[32,512]{1,0:T(8,128)S(1)}, f32[32,512]{1,0:T(8,128)S(1)}, u32[]{:S(2)}, u32[]{:S(2)}) %collective-permute-start.14) | collective-permute-done | bytes 65568 | tf_op jit(solution)/shard_map/ppermute | solution.py:64
  34.1 1.6 %collective-permute-start.15 = (f32[64,512]{1,0:T(8,128)S(1)}, f32[64,512]{1,0:T(8,128)S(1)}, u32[]{:S(2)}, u32[]{:S(2)}) collective-permute-start(f32[64,512]{1,0:T(8,128)S(1)} %pad_maximum_fusion.1.rest_4_), channel_id=1, source_target_pairs={{0,4},{1,3},{2,6},{3,1},{4,0},{5,7},{6,2},{7,5},{8,12},{9,11},{10,... | collective-permute-start | bytes 393224 | tf_op jit(solution)/shard_map/ppermute | solution.py:64
  35.7 0.2 collective-permute-done.5
  35.9 1.6 %collective-permute-start.6 = (f32[64,512]{1,0:T(8,128)S(1)}, f32[64,512]{1,0:T(8,128)S(1)}, u32[]{:S(2)}, u32[]{:S(2)}) collective-permute-start(f32[64,512]{1,0:T(8,128)S(1)} %pad_maximum_fusion.rest_0_), channel_id=1, source_target_pairs={{0,4},{1,3},{2,6},{3,1},{4,0},{5,7},{6,2},{7,5},{8,12},{9,11},{10,... | collective-permute-start | bytes 393224 | tf_op jit(solution)/shard_map/ppermute | solution.py:64
  37.5 0.0 collective-permute-start.16
  37.5 0.5 collective-permute-start.7
  38.0 1.2 %collective-permute-done.15.rest_5_ = f32[64,512]{1,0:T(8,128)S(1)} collective-permute-done((f32[64,512]{1,0:T(8,128)S(1)}, f32[64,512]{1,0:T(8,128)S(1)}, u32[]{:S(2)}, u32[]{:S(2)}) %collective-permute-start.15) | collective-permute-done | bytes 131104 | tf_op jit(solution)/shard_map/ppermute | solution.py:64
  39.2 1.8 %collective-permute-done.6.rest_1_ = f32[64,512]{1,0:T(8,128)S(1)} collective-permute-done((f32[64,512]{1,0:T(8,128)S(1)}, f32[64,512]{1,0:T(8,128)S(1)}, u32[]{:S(2)}, u32[]{:S(2)}) %collective-permute-start.6) | collective-permute-done | bytes 131104 | tf_op jit(solution)/shard_map/ppermute | solution.py:64
  41.0 0.1 copy.6.seeds_ref
  41.1 1.2 %collective-permute-done.8.rest_3_ = f32[64,512]{1,0:T(8,128)S(1)} collective-permute-done((f32[64,512]{1,0:T(8,128)S(1)}, f32[64,512]{1,0:T(8,128)S(1)}, u32[]{:S(2)}, u32[]{:S(2)}) %collective-permute-start.8) | collective-permute-done | bytes 131104 | tf_op jit(solution)/shard_map/ppermute | solution.py:64
  42.3 17.5 %iterate.1 = (f32[128,512]{1,0:T(8,128)}, f32[1,512]{1,0:T(1,128)}) custom-call(s32[512,1]{1,0:T(8,128)S(1)} %copy.6.seeds_ref, f32[64,512]{1,0:T(8,128)S(1)} %pad_maximum_fusion.rest_0_, f32[64,512]{1,0:T(8,128)S(1)} %collective-permute-done.6.rest_1_, f32[64,512]{1,0:T(8,128)S(1)} %collective-permute-done.7.rest_2_, ...), custom_call_target="tpu_custom_call" | custom-call | tf_op jit(solution)/shard_map/iterate/pallas_call | solution.py:312
  (27 shorter events, 0.3 us)
Async XLA Ops:
  0.6 0.7 %copy-start = (s32[1,32,2]{1,2,0:T(2,128)S(1)}, s32[1,32,2]{1,2,0:T(2,128)}, u32[]{:S(2)}) copy-start(s32[1,32,2]{1,2,0:T(2,128)} %param.5) | copy-start | bytes 772
  1.3 39.6 %copy-start.1 = (s32[512]{0:T(512)S(1)}, s32[512]{0:T(512)}, u32[]{:S(2)}) copy-start(s32[512]{0:T(512)} %param.7) | copy-start | bytes 6148
  6.3 1.9 %collective-permute-start.9 = (f32[128,512]{1,0:T(8,128)}, f32[128,512]{1,0:T(8,128)S(1)}, u32[]{:S(2)}, u32[]{:S(2)}) collective-permute-start(f32[128,512]{1,0:T(8,128)} %get-tuple-element.11), channel_id=1, source_target_pairs={{0,1},{1,0},{2,3},{3,2},{4,5},{5,4},{6,7},{7,6},{8,9},{9,8},{10,11... | collective-permute-start | bytes 786440 | tf_op jit(solution)/shard_map/ppermute | solution.py:64
  6.8 4.4 %collective-permute-start = (f32[128,512]{1,0:T(8,128)S(1)}, f32[128,512]{1,0:T(8,128)S(1)}, u32[]{:S(2)}, u32[]{:S(2)}) collective-permute-start(f32[128,512]{1,0:T(8,128)S(1)} %get-tuple-element.9), channel_id=1, source_target_pairs={{0,1},{1,0},{2,3},{3,2},{4,5},{5,4},{6,7},{7,6},{8,9},{9,8},{10,11... | collective-permute-start | bytes 786440 | tf_op jit(solution)/shard_map/ppermute | solution.py:64
  8.3 5.9 %collective-permute-start.10 = (f32[64,512]{1,0:T(8,128)S(1)}, f32[64,512]{1,0:T(8,128)S(1)}, u32[]{:S(2)}, u32[]{:S(2)}) collective-permute-start(f32[64,512]{1,0:T(8,128)S(1)} %slice.37), channel_id=1, source_target_pairs={{0,4},{1,3},{2,6},{3,1},{4,0},{5,7},{6,2},{7,5},{8,12},{9,11},{10,... | collective-permute-start | bytes 393224 | tf_op jit(solution)/shard_map/ppermute | solution.py:64
  11.3 5.0 %collective-permute-start.1 = (f32[64,512]{1,0:T(8,128)S(1)}, f32[64,512]{1,0:T(8,128)S(1)}, u32[]{:S(2)}, u32[]{:S(2)}) collective-permute-start(f32[64,512]{1,0:T(8,128)S(1)} %slice.33), channel_id=1, source_target_pairs={{0,4},{1,3},{2,6},{3,1},{4,0},{5,7},{6,2},{7,5},{8,12},{9,11},{10,... | collective-permute-start | bytes 393224 | tf_op jit(solution)/shard_map/ppermute | solution.py:64
  14.2 4.4 %collective-permute-start.11 = (f32[32,512]{1,0:T(8,128)S(1)}, f32[32,512]{1,0:T(8,128)S(1)}, u32[]{:S(2)}, u32[]{:S(2)}) collective-permute-start(f32[32,512]{1,0:T(8,128)S(1)} %slice.39), channel_id=1, source_target_pairs={{0,2},{1,5},{2,0},{3,7},{4,6},{5,1},{6,4},{7,3},{8,10},{9,13},{10,... | collective-permute-start | bytes 196616 | tf_op jit(solution)/shard_map/ppermute | solution.py:64
  16.3 5.4 %collective-permute-start.2 = (f32[32,512]{1,0:T(8,128)S(1)}, f32[32,512]{1,0:T(8,128)S(1)}, u32[]{:S(2)}, u32[]{:S(2)}) collective-permute-start(f32[32,512]{1,0:T(8,128)S(1)} %slice.35), channel_id=1, source_target_pairs={{0,2},{1,5},{2,0},{3,7},{4,6},{5,1},{6,4},{7,3},{8,10},{9,13},{10,... | collective-permute-start | bytes 196616 | tf_op jit(solution)/shard_map/ppermute | solution.py:64
  18.6 5.4 %collective-permute-start.12 = (f32[32,512]{1,0:T(8,128)S(1)}, f32[32,512]{1,0:T(8,128)S(1)}, u32[]{:S(2)}, u32[]{:S(2)}) collective-permute-start(f32[32,512]{1,0:T(8,128)S(1)} %slice_add_fusion.2), channel_id=1, source_target_pairs={{0,16},{1,17},{2,18},{3,19},{4,20},{5,21},{6,22},{7,23},{8,24},{9,... | collective-permute-start | bytes 196616 | tf_op jit(solution)/shard_map/ppermute | solution.py:64
  21.7 4.3 %collective-permute-start.3 = (f32[32,512]{1,0:T(8,128)S(1)}, f32[32,512]{1,0:T(8,128)S(1)}, u32[]{:S(2)}, u32[]{:S(2)}) collective-permute-start(f32[32,512]{1,0:T(8,128)S(1)} %slice_add_fusion.3), channel_id=1, source_target_pairs={{0,8},{1,9},{2,10},{3,11},{4,12},{5,13},{6,14},{7,15},{8,0},{9,1},... | collective-permute-start | bytes 196616 | tf_op jit(solution)/shard_map/ppermute | solution.py:64
  24.0 5.3 %collective-permute-start.13 = (f32[32,512]{1,0:T(8,128)S(1)}, f32[32,512]{1,0:T(8,128)S(1)}, u32[]{:S(2)}, u32[]{:S(2)}) collective-permute-start(f32[32,512]{1,0:T(8,128)S(1)} %add.38), channel_id=1, source_target_pairs={{0,8},{1,9},{2,10},{3,11},{4,12},{5,13},{6,14},{7,15},{8,0},{9,1},... | collective-permute-start | bytes 196616 | tf_op jit(solution)/shard_map/ppermute | solution.py:64
  26.1 5.5 %collective-permute-start.4 = (f32[32,512]{1,0:T(8,128)S(1)}, f32[32,512]{1,0:T(8,128)S(1)}, u32[]{:S(2)}, u32[]{:S(2)}) collective-permute-start(f32[32,512]{1,0:T(8,128)S(1)} %add.33), channel_id=1, source_target_pairs={{0,16},{1,17},{2,18},{3,19},{4,20},{5,21},{6,22},{7,23},{8,24},{9,... | collective-permute-start | bytes 196616 | tf_op jit(solution)/shard_map/ppermute | solution.py:64
  29.3 4.8 %collective-permute-start.14 = (f32[32,512]{1,0:T(8,128)S(1)}, f32[32,512]{1,0:T(8,128)S(1)}, u32[]{:S(2)}, u32[]{:S(2)}) collective-permute-start(f32[32,512]{1,0:T(8,128)S(1)} %add.39), channel_id=1, source_target_pairs={{0,2},{1,5},{2,0},{3,7},{4,6},{5,1},{6,4},{7,3},{8,10},{9,13},{10,... | collective-permute-start | bytes 196616 | tf_op jit(solution)/shard_map/ppermute | solution.py:64
  31.6 4.3 %collective-permute-start.5 = (f32[32,512]{1,0:T(8,128)S(1)}, f32[32,512]{1,0:T(8,128)S(1)}, u32[]{:S(2)}, u32[]{:S(2)}) collective-permute-start(f32[32,512]{1,0:T(8,128)S(1)} %add.34), channel_id=1, source_target_pairs={{0,2},{1,5},{2,0},{3,7},{4,6},{5,1},{6,4},{7,3},{8,10},{9,13},{10,... | collective-permute-start | bytes 196616 | tf_op jit(solution)/shard_map/ppermute | solution.py:64
  34.1 5.0 %collective-permute-start.15 = (f32[64,512]{1,0:T(8,128)S(1)}, f32[64,512]{1,0:T(8,128)S(1)}, u32[]{:S(2)}, u32[]{:S(2)}) collective-permute-start(f32[64,512]{1,0:T(8,128)S(1)} %pad_maximum_fusion.1.rest_4_), channel_id=1, source_target_pairs={{0,4},{1,3},{2,6},{3,1},{4,0},{5,7},{6,2},{7,5},{8,12},{9,11},{10,... | collective-permute-start | bytes 393224 | tf_op jit(solution)/shard_map/ppermute | solution.py:64
  35.9 5.0 %collective-permute-start.6 = (f32[64,512]{1,0:T(8,128)S(1)}, f32[64,512]{1,0:T(8,128)S(1)}, u32[]{:S(2)}, u32[]{:S(2)}) collective-permute-start(f32[64,512]{1,0:T(8,128)S(1)} %pad_maximum_fusion.rest_0_), channel_id=1, source_target_pairs={{0,4},{1,3},{2,6},{3,1},{4,0},{5,7},{6,2},{7,5},{8,12},{9,11},{10,... | collective-permute-start | bytes 393224 | tf_op jit(solution)/shard_map/ppermute | solution.py:64
  37.5 3.6 %collective-permute-start.16 = (f32[64,512]{1,0:T(8,128)S(1)}, f32[64,512]{1,0:T(8,128)S(1)}, u32[]{:S(2)}, u32[]{:S(2)}) collective-permute-start(f32[64,512]{1,0:T(8,128)S(1)} %pad_maximum_fusion.1.rest_4_), channel_id=1, source_target_pairs={{0,1},{1,0},{2,3},{3,2},{4,5},{5,4},{6,7},{7,6},{8,9},{9,8},{10,11... | collective-permute-start | bytes 393224 | tf_op jit(solution)/shard_map/ppermute | solution.py:64
  37.5 3.6 %collective-permute-start.7 = (f32[64,512]{1,0:T(8,128)S(1)}, f32[64,512]{1,0:T(8,128)S(1)}, u32[]{:S(2)}, u32[]{:S(2)}) collective-permute-start(f32[64,512]{1,0:T(8,128)S(1)} %pad_maximum_fusion.rest_0_), channel_id=1, source_target_pairs={{0,1},{1,0},{2,3},{3,2},{4,5},{5,4},{6,7},{7,6},{8,9},{9,8},{10,11... | collective-permute-start | bytes 393224 | tf_op jit(solution)/shard_map/ppermute | solution.py:64
  39.2 2.0 %collective-permute-start.17 = (f32[64,512]{1,0:T(8,128)S(1)}, f32[64,512]{1,0:T(8,128)S(1)}, u32[]{:S(2)}, u32[]{:S(2)}) collective-permute-start(f32[64,512]{1,0:T(8,128)S(1)} %collective-permute-done.15.rest_5_), channel_id=1, source_target_pairs={{0,1},{1,0},{2,3},{3,2},{4,5},{5,4},{6,7},{7,6},{8,9},{9,8},{10,11... | collective-permute-start | bytes 393224 | tf_op jit(solution)/shard_map/ppermute | solution.py:64
  40.9 1.3 %collective-permute-start.8 = (f32[64,512]{1,0:T(8,128)S(1)}, f32[64,512]{1,0:T(8,128)S(1)}, u32[]{:S(2)}, u32[]{:S(2)}) collective-permute-start(f32[64,512]{1,0:T(8,128)S(1)} %collective-permute-done.6.rest_1_), channel_id=1, source_target_pairs={{0,1},{1,0},{2,3},{3,2},{4,5},{5,4},{6,7},{7,6},{8,9},{9,8},{10,11... | collective-permute-start | bytes 393224 | tf_op jit(solution)/shard_map/ppermute | solution.py:64
